TPU v7x, 32 devices: a whole 2x2x4 slice. The times are simulated.
32 devices in a mesh: gx: 8 (over z, y), gy: 4 (over x, core).
Axes of the slice: x: 2, y: 2, z: 4, core: 2. Of those that a mesh axis runs over, the one named last changes fastest.
Arguments:
- adjoint_trace: bfloat16 [128, 64, 16, 128], P('gx', 'gy'), may hold values from -6 to 6
- coupling: bfloat16 [7, 128, 128], replicated, may hold values from -0.1875 to 0.1875
- log_friction: float32 [64, 64, 128], P('gx', 'gy'), may hold values from -1 to 1
- send_column: int32 [8, 4, 256], P('gx', 'gy'), may hold values from 0 to 255, each once within a row
- live_count: int32 [8, 4, 4], P('gx', 'gy'), may hold values from 0 to 64, as said below
- target_node: int32 [8, 4, 4, 64], P('gx', 'gy'), may hold values from 0 to 127
Outputs:
- trace_update: bfloat16 [128, 64, 16, 128], P('gx', 'gy')
- friction_gradient: float32 [64, 64, 128], P('gx', 'gy')
Inputs may be any that keep to these rules, and one draw needn't show every extreme that they name: Each row of send_column lists every local basal face once. `live_count`: in every row of devices along gy, one owner receives 64 live blocks from every device.
All inputs are finite; a program needn't handle non-finite values.
Results may differ from a plain program's by a relative error of at most 0.0059.
Values may be sent and summed in bfloat16 or wider, within the bound.
A program may use at most 64 MiB of HBM per device.

v0:
```python
import jax
import jax.numpy as jnp
from jax import lax
from jax.sharding import PartitionSpec as P


def padded_2(block, sides, width):
    for axis, dim in sides:
        count = lax.axis_size(axis)
        forward = [(i, i + 1) for i in range(count - 1)]
        backward = [(target, source) for source, target in forward]
        low = lax.ppermute(
            lax.slice_in_dim(block, block.shape[dim] - width, None, axis=dim), axis, forward
        )
        high = lax.ppermute(lax.slice_in_dim(block, 0, width, axis=dim), axis, backward)
        block = jnp.concatenate([low, block, high], axis=dim)
    return block


def couple(extended, coupling):
    own = extended[1:-1, 1:-1]
    rows_a, rows_b, layers_n, width = own.shape
    zeros_layer = jnp.zeros((rows_a, rows_b, 1, width), jnp.bfloat16)
    below = jnp.concatenate([zeros_layer, own[:, :, :-1]], axis=2)
    above = jnp.concatenate([own[:, :, 1:], zeros_layer], axis=2)
    terms = [
        own,
        below,
        above,
        extended[:-2, 1:-1],
        extended[2:, 1:-1],
        extended[1:-1, :-2],
        extended[1:-1, 2:],
    ]
    total = jnp.zeros((rows_a * rows_b * layers_n, width), jnp.float32)
    for index in range(7):
        total = total + jnp.dot(
            terms[index].reshape(-1, width), coupling[index], preferred_element_type=jnp.float32
        )
    return total.reshape(rows_a, rows_b, layers_n, width).astype(jnp.bfloat16)


def stencil(extended):
    center = extended[1:-1, 1:-1]
    beside_all = extended[2:, 1:-1] + extended[:-2, 1:-1] + extended[1:-1, 2:] + extended[1:-1, :-2]
    return 1.3 * center - 0.2 * beside_all


def prior_once(field):
    extended = padded_2(field.astype(jnp.bfloat16), (("gx", 0), ("gy", 1)), 1).astype(field.dtype)
    return stencil(extended)


def per_device(adjoint_trace, coupling, log_friction, send_column, live_count, target_node):
    rows_a, rows_b, layers_n, width = adjoint_trace.shape
    padded = padded_2(adjoint_trace, (("gx", 0), ("gy", 1)), 1)
    trace_update = couple(padded, coupling)
    owners = lax.axis_size("gy")
    faces_dev = rows_a * rows_b
    slots = faces_dev // owners
    blocks_all = trace_update[:, :, 0, :].reshape(faces_dev, width)
    order = send_column.reshape(owners, slots)
    picked = blocks_all[order]
    live = jnp.arange(slots, dtype=jnp.int32)[None, :] < live_count.reshape(owners)[:, None]
    nodes = jnp.where(live, target_node.reshape(owners, slots), -1)
    received, received_nodes = (
        lax.all_to_all(picked, "gy", split_axis=0, concat_axis=0, tiled=True),
        lax.all_to_all(nodes, "gy", split_axis=0, concat_axis=0, tiled=True),
    )
    tile_a, tile_b = (log_friction.shape[0], log_friction.shape[1])
    tile_nodes = tile_a * tile_b
    onehot = (
        jnp.arange(tile_nodes, dtype=jnp.int32)[:, None] == received_nodes.reshape(-1)[None, :]
    ).astype(jnp.bfloat16)
    misfit = jnp.dot(
        onehot, received.reshape(-1, width), preferred_element_type=jnp.float32
    ).reshape(tile_a, tile_b, width)
    prior = prior_once(prior_once(log_friction))
    friction_gradient = jnp.exp(log_friction) * misfit + prior
    return (trace_update, friction_gradient)


def solution(mesh):
    in_specs = (
        P("gx", "gy", None, None),
        P(),
        P("gx", "gy", None),
        P("gx", "gy", None),
        P("gx", "gy", None),
        P("gx", "gy", None, None),
    )
    out_specs = (P("gx", "gy", None, None), P("gx", "gy", None))
    return jax.shard_map(
        per_device, mesh=mesh, in_specs=in_specs, out_specs=out_specs, check_vma=False
    )
```

profile of v0, /device:TPU:0, one launch (start us, length us, event | category | flops | bytes accessed | tf_op | source)
XLA Modules:
  0.0 76.1 jit_solution(10322667185749115808)
XLA Ops:
  0.6 0.8 %convert_element_type.21 = bf16[8,16,128]{2,1,0:T(8,128)(2,1)S(1)} convert(f32[8,16,128]{2,1,0:T(8,128)} %param.8) | non-fusion elementwise | flops 16384 | bytes 98304 | tf_op jit(solution)/shard_map/convert_element_type | solution.py:50
  1.5 0.6 fusion.35
  2.1 4.9 %collective-permute-start.4 = (bf16[1,16,128]{2,1,0:T(8,128)(2,1)}, bf16[1,16,128]{2,1,0:T(8,128)(2,1)S(1)}, u32[]{:S(2)}, u32[]{:S(2)}) collective-permute-start(bf16[1,16,128]{2,1,0:T(8,128)(2,1)} %get-tuple-element.19), channel_id=1, source_target_pairs={{0,4},{4,8},{8,12},{12,16},{16,20},{20,24},{24,28},{1,5},{5,9},{9,... | collective-permute-start | bytes 12296 | tf_op jit(solution)/shard_map/ppermute | solution.py:12
  6.9 1.3 %collective-permute-start.5 = (bf16[1,16,128]{2,1,0:T(8,128)(2,1)}, bf16[1,16,128]{2,1,0:T(8,128)(2,1)S(1)}, u32[]{:S(2)}, u32[]{:S(2)}) collective-permute-start(bf16[1,16,128]{2,1,0:T(8,128)(2,1)} %get-tuple-element.20), channel_id=1, source_target_pairs={{4,0},{8,4},{12,8},{16,12},{20,16},{24,20},{28,24},{5,1},{9,5},{13... | collective-permute-start | bytes 12296 | tf_op jit(solution)/shard_map/ppermute | solution.py:15
  8.2 1.5 %fusion.33 = (bf16[1,16,16,128]{3,2,1,0:T(8,128)(2,1)}, bf16[1,16,16,128]{3,2,1,0:T(8,128)(2,1)}) fusion(bf16[16,16,16,128]{3,2,1,0:T(8,128)(2,1)} %param.6), kind=kLoop, calls=%fused_computation.65 | loop fusion | bytes 262144 | tf_op jit(solution)/shard_map/slice | solution.py:15
  9.8 4.5 %collective-permute-start = (bf16[1,16,16,128]{3,2,1,0:T(8,128)(2,1)}, bf16[1,16,16,128]{3,2,1,0:T(8,128)(2,1)S(1)}, u32[]{:S(2)}, u32[]{:S(2)}) collective-permute-start(bf16[1,16,16,128]{3,2,1,0:T(8,128)(2,1)} %get-tuple-element.12), channel_id=1, source_target_pairs={{0,4},{4,8},{8,12},{12,16},{16,20},{20,24},{24,28},{1,5},{5,9},{9,... | collective-permute-start | bytes 196616 | tf_op jit(solution)/shard_map/ppermute | solution.py:12
  14.3 1.3 %collective-permute-start.1 = (bf16[1,16,16,128]{3,2,1,0:T(8,128)(2,1)}, bf16[1,16,16,128]{3,2,1,0:T(8,128)(2,1)S(1)}, u32[]{:S(2)}, u32[]{:S(2)}) collective-permute-start(bf16[1,16,16,128]{3,2,1,0:T(8,128)(2,1)} %get-tuple-element.11), channel_id=1, source_target_pairs={{4,0},{8,4},{12,8},{16,12},{20,16},{24,20},{28,24},{5,1},{9,5},{13... | collective-permute-start | bytes 196616 | tf_op jit(solution)/shard_map/ppermute | solution.py:15
  15.6 1.3 %compare_select_fusion = s32[4,1,64]{2,1,0:T(1,128)} fusion(s32[4,1,64]{2,1,0:T(1,128)} %bitcast.57, s32[4]{0:T(128)} %bitcast.58), kind=kLoop, calls=%fused_computation.50 | loop fusion | flops 512 | bytes 2064 | tf_op jit(solution)/shard_map/jit(_where)/select_n | solution.py:65
  16.9 3.2 %all-to-all-start = ((s32[4,1,64]{2,1,0:T(1,128)}), s32[4,1,64]{2,1,0:T(1,128)S(1)}, u32[]{:S(2)}, u32[]{:S(2)}) async-start(s32[4,1,64]{2,1,0:T(1,128)} %compare_select_fusion), calls=%async_computation | async-start | bytes 4096 | tf_op jit(solution)/shard_map/all_to_all | solution.py:68
  20.1 2.2 %fusion.32 = (bf16[16,16,15,128]{3,2,1,0:T(8,128)(2,1)S(1)}, bf16[16,16,15,128]{3,2,1,0:T(8,128)(2,1)S(1)}) fusion(bf16[16,16,16,128]{3,2,1,0:T(8,128)(2,1)} %param.6), kind=kLoop, calls=%fused_computation.64 | loop fusion | bytes 3932160 | tf_op jit(solution)/shard_map/slice | solution.py:25
  22.3 0.0 copy-start.7
  22.3 0.0 copy-start
  22.3 0.0 copy-start.3
  22.3 0.4 concatenate.34
  22.8 1.2 %concatenate.35 = bf16[16,16,16,128]{3,2,1,0:T(8,128)(2,1)} pad(bf16[16,16,15,128]{3,2,1,0:T(8,128)(2,1)S(1)} %get-tuple-element.9, bf16[]{:T(256)} %constant.1.clone.1), padding=0_0x0_0x0_1x0_0 | pad | bytes 2031618 | tf_op jit(solution)/shard_map/concatenate | solution.py:25
  24.0 0.6 broadcast.82
  24.6 0.7 reduce.6
  25.3 0.7 reshape.143
  26.0 0.4 fusion.22
  26.4 0.0 copy-start.1
  26.4 0.4 convolution_add_fusion.2
  26.8 0.8 %copy-done.1 = bf16[16,16,16,128]{3,2,1,0:T(8,128)(2,1)S(1)} copy-done((bf16[16,16,16,128]{3,2,1,0:T(8,128)(2,1)S(1)}, bf16[16,16,16,128]{3,2,1,0:T(8,128)(2,1)}, u32[]{:S(2)}) %copy-start.1) | copy-done | bytes 1048600
  27.6 0.4 convolution_add_fusion.1
  28.0 0.2 copy-done.5
  28.3 0.6 pad_maximum_fusion.9
  28.9 3.0 %collective-permute-start.6 = (bf16[10,1,128]{2,1,0:T(2,128)(2,1)}, bf16[10,1,128]{2,1,0:T(2,128)(2,1)}, u32[]{:S(2)}, u32[]{:S(2)}) collective-permute-start(bf16[10,1,128]{2,1,0:T(2,128)(2,1)} %get-tuple-element.15), channel_id=1, source_target_pairs={{0,1},{1,2},{2,3},{4,5},{5,6},{6,7},{8,9},{9,10},{10,11},{12,13},{... | collective-permute-start | bytes 7688 | tf_op jit(solution)/shard_map/ppermute | solution.py:12
  31.9 1.3 %collective-permute-start.7 = (bf16[10,1,128]{2,1,0:T(2,128)(2,1)}, bf16[10,1,128]{2,1,0:T(2,128)(2,1)}, u32[]{:S(2)}, u32[]{:S(2)}) collective-permute-start(bf16[10,1,128]{2,1,0:T(2,128)(2,1)} %get-tuple-element.16), channel_id=1, source_target_pairs={{1,0},{2,1},{3,2},{5,4},{6,5},{7,6},{9,8},{10,9},{11,10},{13,12},{... | collective-permute-start | bytes 7688 | tf_op jit(solution)/shard_map/ppermute | solution.py:15
  33.1 0.6 multiply_add_fusion
  33.7 0.7 reshape.147
  34.4 1.4 %collective-permute-done.7 = bf16[10,1,128]{2,1,0:T(2,128)(2,1)} collective-permute-done((bf16[10,1,128]{2,1,0:T(2,128)(2,1)}, bf16[10,1,128]{2,1,0:T(2,128)(2,1)}, u32[]{:S(2)}, u32[]{:S(2)}) %collective-permute-start.7) | collective-permute-done | bytes 2592 | tf_op jit(solution)/shard_map/ppermute | solution.py:15
  35.8 0.7 maximum_convert_fusion
  36.6 0.6 fusion.34
  37.2 4.9 %collective-permute-start.8 = (bf16[1,16,128]{2,1,0:T(8,128)(2,1)}, bf16[1,16,128]{2,1,0:T(8,128)(2,1)S(1)}, u32[]{:S(2)}, u32[]{:S(2)}) collective-permute-start(bf16[1,16,128]{2,1,0:T(8,128)(2,1)} %get-tuple-element.17), channel_id=1, source_target_pairs={{0,4},{4,8},{8,12},{12,16},{16,20},{20,24},{24,28},{1,5},{5,9},{9,... | collective-permute-start | bytes 12296 | tf_op jit(solution)/shard_map/ppermute | solution.py:12
  42.1 1.3 %collective-permute-start.9 = (bf16[1,16,128]{2,1,0:T(8,128)(2,1)}, bf16[1,16,128]{2,1,0:T(8,128)(2,1)S(1)}, u32[]{:S(2)}, u32[]{:S(2)}) collective-permute-start(bf16[1,16,128]{2,1,0:T(8,128)(2,1)} %get-tuple-element.18), channel_id=1, source_target_pairs={{4,0},{8,4},{12,8},{16,12},{20,16},{24,20},{28,24},{5,1},{9,5},{13... | collective-permute-start | bytes 12296 | tf_op jit(solution)/shard_map/ppermute | solution.py:15
  43.4 0.7 pad_clamp_fusion
  44.1 0.0 all-to-all-done
  44.1 1.3 %reduce.7 = s32[4,64]{1,0:T(4,128)} reduce(s32[4,1,64]{2,1,0:T(1,128)S(1)} %all-to-all-done, s32[]{:T(128)} %broadcast.82), dimensions={1}, to_apply=%all_to_all.7.reduce_sub_computation.3 | reduce | bytes 2052 | tf_op jit(solution)/shard_map/all_to_all | solution.py:68
  45.4 0.8 eq.30
  46.1 0.0 collective-permute-done.8
  46.1 2.6 %collective-permute-done.9 = bf16[1,16,128]{2,1,0:T(8,128)(2,1)S(1)} collective-permute-done((bf16[1,16,128]{2,1,0:T(8,128)(2,1)}, bf16[1,16,128]{2,1,0:T(8,128)(2,1)S(1)}, u32[]{:S(2)}, u32[]{:S(2)}) %collective-permute-start.9) | collective-permute-done | bytes 4128 | tf_op jit(solution)/shard_map/ppermute | solution.py:15
  48.7 0.6 pad_maximum_fusion.6
  49.4 3.7 %collective-permute-start.10 = (bf16[10,1,128]{2,1,0:T(2,128)(2,1)}, bf16[10,1,128]{2,1,0:T(2,128)(2,1)}, u32[]{:S(2)}, u32[]{:S(2)}) collective-permute-start(bf16[10,1,128]{2,1,0:T(2,128)(2,1)} %get-tuple-element.13), channel_id=1, source_target_pairs={{0,1},{1,2},{2,3},{4,5},{5,6},{6,7},{8,9},{9,10},{10,11},{12,13},{... | collective-permute-start | bytes 7688 | tf_op jit(solution)/shard_map/ppermute | solution.py:12
  53.0 1.3 %collective-permute-start.11 = (bf16[10,1,128]{2,1,0:T(2,128)(2,1)}, bf16[10,1,128]{2,1,0:T(2,128)(2,1)}, u32[]{:S(2)}, u32[]{:S(2)}) collective-permute-start(bf16[10,1,128]{2,1,0:T(2,128)(2,1)} %get-tuple-element.14), channel_id=1, source_target_pairs={{1,0},{2,1},{3,2},{5,4},{6,5},{7,6},{9,8},{10,9},{11,10},{13,12},{... | collective-permute-start | bytes 7688 | tf_op jit(solution)/shard_map/ppermute | solution.py:15
  54.3 0.0 collective-permute-done
  54.3 0.0 collective-permute-done.1
  54.4 0.7 pad_maximum_fusion.3
  55.1 3.1 %collective-permute-start.2 = (bf16[18,1,16,128]{3,2,1,0:T(8,128)(2,1)S(1)}, bf16[18,1,16,128]{3,2,1,0:T(8,128)(2,1)S(1)}, u32[]{:S(2)}, u32[]{:S(2)}) collective-permute-start(bf16[18,1,16,128]{3,2,1,0:T(8,128)(2,1)S(1)} %get-tuple-element.4), channel_id=1, source_target_pairs={{0,1},{1,2},{2,3},{4,5},{5,6},{6,7},{8,9},{9,10},{10,11},{12,13},{... | collective-permute-start | bytes 221192 | tf_op jit(solution)/shard_map/ppermute | solution.py:12
  58.1 1.3 %collective-permute-start.3 = (bf16[18,1,16,128]{3,2,1,0:T(8,128)(2,1)S(1)}, bf16[18,1,16,128]{3,2,1,0:T(8,128)(2,1)S(1)}, u32[]{:S(2)}, u32[]{:S(2)}) collective-permute-start(bf16[18,1,16,128]{3,2,1,0:T(8,128)(2,1)S(1)} %get-tuple-element.5), channel_id=1, source_target_pairs={{1,0},{2,1},{3,2},{5,4},{6,5},{7,6},{9,8},{10,9},{11,10},{13,12},{... | collective-permute-start | bytes 221192 | tf_op jit(solution)/shard_map/ppermute | solution.py:15
  59.4 0.4 fusion.17
  59.9 0.0 collective-permute-done.2
  59.9 2.7 %collective-permute-done.3 = bf16[18,1,16,128]{3,2,1,0:T(8,128)(2,1)S(1)} collective-permute-done((bf16[18,1,16,128]{3,2,1,0:T(8,128)(2,1)S(1)}, bf16[18,1,16,128]{3,2,1,0:T(8,128)(2,1)S(1)}, u32[]{:S(2)}, u32[]{:S(2)}) %collective-permute-start.3) | collective-permute-done | bytes 73760 | tf_op jit(solution)/shard_map/ppermute | solution.py:15
  62.5 0.1 pad_maximum_fusion.1
  62.7 0.4 fusion.13
  63.1 0.4 fusion.15
  63.5 0.0 copy-start.4
  63.5 0.8 %fusion.3 = bf16[4096,128]{1,0:T(8,128)(2,1)S(1)} fusion(f32[4096,128]{1,0:T(8,128)S(1)} %fusion.13, f32[4096,128]{1,0:T(8,128)S(1)} %fusion.15, f32[4096,128]{1,0:T(8,128)S(1)} %fusion.17, f32[4096,128]{1,0:T(8,128)S(1)} %convolution_add_fusion.1, bf16[4096,128]{1,0:T(8,128)(2,1)S(1)} %bitcast.52, bf16[7,128,128]{2,1,0:T(8,128)(2,1)S(1)} %copy-done.3), kind=kOutput, calls=%fused_computation.7 | convolution fusion | flops 136839168 | bytes 10518528 | tf_op jit(solution)/shard_map/dot_general | solution.py:37
  64.3 0.0 copy-start.2
  64.3 1.0 %copy-done.2 = bf16[4096,128]{1,0:T(8,128)(2,1)} copy-done((bf16[4096,128]{1,0:T(8,128)(2,1)}, bf16[4096,128]{1,0:T(8,128)(2,1)S(1)}, u32[]{:S(2)}) %copy-start.2) | copy-done | bytes 1048600
  65.3 0.1 slice.152
  65.4 1.5 %gather_fusion = bf16[256,128]{1,0:T(8,128)(2,1)} fusion(bf16[256,128]{1,0:T(8,128)(2,1)S(1)} %bitcast.47, s32[1024]{0:T(1024)S(1)} %pad_clamp_fusion), kind=kCustom, calls=%fused_computation | custom fusion | bytes 132096 | tf_op jit(solution)/shard_map/gather | solution.py:63
  66.9 4.3 %all-to-all-start.1 = ((bf16[4,64,128]{2,1,0:T(8,128)(2,1)}), bf16[4,64,128]{2,1,0:T(8,128)(2,1)S(1)}, u32[]{:S(2)}, u32[]{:S(2)}) async-start(bf16[4,64,128]{2,1,0:T(8,128)(2,1)} %bitcast.18), calls=%async_computation.1 | async-start | bytes 131072 | tf_op jit(solution)/shard_map/all_to_all | solution.py:67
  71.1 0.7 maximum_convert_fusion.1
  71.9 3.4 %all-to-all-done.1 = bf16[4,64,128]{2,1,0:T(8,128)(2,1)S(1)} async-done(((bf16[4,64,128]{2,1,0:T(8,128)(2,1)}), bf16[4,64,128]{2,1,0:T(8,128)(2,1)S(1)}, u32[]{:S(2)}, u32[]{:S(2)}) %all-to-all-start.1) | async-done | bytes 65568 | tf_op jit(solution)/shard_map/all_to_all | solution.py:67
  75.3 0.8 %fusion.4 = f32[8,16,128]{2,1,0:T(8,128)} fusion(bf16[256,128,1]{1,0,2:T(8,128)(2,1)S(1)} %bitcast.56, f32[10,18,128]{2,1,0:T(8,128)S(1)} %maximum_convert_fusion.1, s32[256]{0:T(256)S(1)} %eq.30, s32[8,16]{1,0:T(8,128)S(1)} %copy-done.6, f32[8,16,128]{2,1,0:T(8,128)S(1)} %copy-done.4), kind=kOutput, calls=%fused_computation.9 | convolution fusion | flops 8552448 | bytes 525824 | tf_op jit(solution)/shard_map/dot_general | solution.py:75
  (18 shorter events, 0.1 us)
Async XLA Ops:
  2.1 26.2 %collective-permute-start.4 = (bf16[1,16,128]{2,1,0:T(8,128)(2,1)}, bf16[1,16,128]{2,1,0:T(8,128)(2,1)S(1)}, u32[]{:S(2)}, u32[]{:S(2)}) collective-permute-start(bf16[1,16,128]{2,1,0:T(8,128)(2,1)} %get-tuple-element.19), channel_id=1, source_target_pairs={{0,4},{4,8},{8,12},{12,16},{16,20},{20,24},{24,28},{1,5},{5,9},{9,... | collective-permute-start | bytes 12296 | tf_op jit(solution)/shard_map/ppermute | solution.py:12
  6.9 21.3 %collective-permute-start.5 = (bf16[1,16,128]{2,1,0:T(8,128)(2,1)}, bf16[1,16,128]{2,1,0:T(8,128)(2,1)S(1)}, u32[]{:S(2)}, u32[]{:S(2)}) collective-permute-start(bf16[1,16,128]{2,1,0:T(8,128)(2,1)} %get-tuple-element.20), channel_id=1, source_target_pairs={{4,0},{8,4},{12,8},{16,12},{20,16},{24,20},{28,24},{5,1},{9,5},{13... | collective-permute-start | bytes 12296 | tf_op jit(solution)/shard_map/ppermute | solution.py:15
  9.8 44.6 %collective-permute-start = (bf16[1,16,16,128]{3,2,1,0:T(8,128)(2,1)}, bf16[1,16,16,128]{3,2,1,0:T(8,128)(2,1)S(1)}, u32[]{:S(2)}, u32[]{:S(2)}) collective-permute-start(bf16[1,16,16,128]{3,2,1,0:T(8,128)(2,1)} %get-tuple-element.12), channel_id=1, source_target_pairs={{0,4},{4,8},{8,12},{12,16},{16,20},{20,24},{24,28},{1,5},{5,9},{9,... | collective-permute-start | bytes 196616 | tf_op jit(solution)/shard_map/ppermute | solution.py:12
  14.3 40.0 %collective-permute-start.1 = (bf16[1,16,16,128]{3,2,1,0:T(8,128)(2,1)}, bf16[1,16,16,128]{3,2,1,0:T(8,128)(2,1)S(1)}, u32[]{:S(2)}, u32[]{:S(2)}) collective-permute-start(bf16[1,16,16,128]{3,2,1,0:T(8,128)(2,1)} %get-tuple-element.11), channel_id=1, source_target_pairs={{4,0},{8,4},{12,8},{16,12},{20,16},{24,20},{28,24},{5,1},{9,5},{13... | collective-permute-start | bytes 196616 | tf_op jit(solution)/shard_map/ppermute | solution.py:15
  16.9 27.2 %all-to-all-start = ((s32[4,1,64]{2,1,0:T(1,128)}), s32[4,1,64]{2,1,0:T(1,128)S(1)}, u32[]{:S(2)}, u32[]{:S(2)}) async-start(s32[4,1,64]{2,1,0:T(1,128)} %compare_select_fusion), calls=%async_computation | async-start | bytes 4096 | tf_op jit(solution)/shard_map/all_to_all | solution.py:68
  22.3 2.3 %copy-start.7 = (s32[1,1,256]{2,1,0:T(1,128)S(1)}, s32[1,1,256]{2,1,0:T(1,128)}, u32[]{:S(2)}) copy-start(s32[1,1,256]{2,1,0:T(1,128)} %param.9) | copy-start | bytes 3076
  22.3 3.6 %copy-start = (bf16[16,16,16,128]{3,2,1,0:T(8,128)(2,1)S(1)}, bf16[16,16,16,128]{3,2,1,0:T(8,128)(2,1)}, u32[]{:S(2)}) copy-start(bf16[16,16,16,128]{3,2,1,0:T(8,128)(2,1)} %param.6) | copy-start | bytes 3145732
  22.3 3.6 %copy-start.3 = (bf16[7,128,128]{2,1,0:T(8,128)(2,1)S(1)}, bf16[7,128,128]{2,1,0:T(8,128)(2,1)}, u32[]{:S(2)}) copy-start(bf16[7,128,128]{2,1,0:T(8,128)(2,1)} %param.7) | copy-start | bytes 688132
  26.4 1.2 %copy-start.1 = (bf16[16,16,16,128]{3,2,1,0:T(8,128)(2,1)S(1)}, bf16[16,16,16,128]{3,2,1,0:T(8,128)(2,1)}, u32[]{:S(2)}) copy-start(bf16[16,16,16,128]{3,2,1,0:T(8,128)(2,1)} %concatenate.35) | copy-start | bytes 3145732
  27.6 0.7 copy-start.5
  28.9 5.5 %collective-permute-start.6 = (bf16[10,1,128]{2,1,0:T(2,128)(2,1)}, bf16[10,1,128]{2,1,0:T(2,128)(2,1)}, u32[]{:S(2)}, u32[]{:S(2)}) collective-permute-start(bf16[10,1,128]{2,1,0:T(2,128)(2,1)} %get-tuple-element.15), channel_id=1, source_target_pairs={{0,1},{1,2},{2,3},{4,5},{5,6},{6,7},{8,9},{9,10},{10,11},{12,13},{... | collective-permute-start | bytes 7688 | tf_op jit(solution)/shard_map/ppermute | solution.py:12
  31.9 4.0 %collective-permute-start.7 = (bf16[10,1,128]{2,1,0:T(2,128)(2,1)}, bf16[10,1,128]{2,1,0:T(2,128)(2,1)}, u32[]{:S(2)}, u32[]{:S(2)}) collective-permute-start(bf16[10,1,128]{2,1,0:T(2,128)(2,1)} %get-tuple-element.16), channel_id=1, source_target_pairs={{1,0},{2,1},{3,2},{5,4},{6,5},{7,6},{9,8},{10,9},{11,10},{13,12},{... | collective-permute-start | bytes 7688 | tf_op jit(solution)/shard_map/ppermute | solution.py:15
  37.2 9.0 %collective-permute-start.8 = (bf16[1,16,128]{2,1,0:T(8,128)(2,1)}, bf16[1,16,128]{2,1,0:T(8,128)(2,1)S(1)}, u32[]{:S(2)}, u32[]{:S(2)}) collective-permute-start(bf16[1,16,128]{2,1,0:T(8,128)(2,1)} %get-tuple-element.17), channel_id=1, source_target_pairs={{0,4},{4,8},{8,12},{12,16},{16,20},{20,24},{24,28},{1,5},{5,9},{9,... | collective-permute-start | bytes 12296 | tf_op jit(solution)/shard_map/ppermute | solution.py:12
  42.1 6.6 %collective-permute-start.9 = (bf16[1,16,128]{2,1,0:T(8,128)(2,1)}, bf16[1,16,128]{2,1,0:T(8,128)(2,1)S(1)}, u32[]{:S(2)}, u32[]{:S(2)}) collective-permute-start(bf16[1,16,128]{2,1,0:T(8,128)(2,1)} %get-tuple-element.18), channel_id=1, source_target_pairs={{4,0},{8,4},{12,8},{16,12},{20,16},{24,20},{28,24},{5,1},{9,5},{13... | collective-permute-start | bytes 12296 | tf_op jit(solution)/shard_map/ppermute | solution.py:15
  49.4 21.8 %collective-permute-start.10 = (bf16[10,1,128]{2,1,0:T(2,128)(2,1)}, bf16[10,1,128]{2,1,0:T(2,128)(2,1)}, u32[]{:S(2)}, u32[]{:S(2)}) collective-permute-start(bf16[10,1,128]{2,1,0:T(2,128)(2,1)} %get-tuple-element.13), channel_id=1, source_target_pairs={{0,1},{1,2},{2,3},{4,5},{5,6},{6,7},{8,9},{9,10},{10,11},{12,13},{... | collective-permute-start | bytes 7688 | tf_op jit(solution)/shard_map/ppermute | solution.py:12
  53.0 18.1 %collective-permute-start.11 = (bf16[10,1,128]{2,1,0:T(2,128)(2,1)}, bf16[10,1,128]{2,1,0:T(2,128)(2,1)}, u32[]{:S(2)}, u32[]{:S(2)}) collective-permute-start(bf16[10,1,128]{2,1,0:T(2,128)(2,1)} %get-tuple-element.14), channel_id=1, source_target_pairs={{1,0},{2,1},{3,2},{5,4},{6,5},{7,6},{9,8},{10,9},{11,10},{13,12},{... | collective-permute-start | bytes 7688 | tf_op jit(solution)/shard_map/ppermute | solution.py:15
  55.1 4.8 %collective-permute-start.2 = (bf16[18,1,16,128]{3,2,1,0:T(8,128)(2,1)S(1)}, bf16[18,1,16,128]{3,2,1,0:T(8,128)(2,1)S(1)}, u32[]{:S(2)}, u32[]{:S(2)}) collective-permute-start(bf16[18,1,16,128]{3,2,1,0:T(8,128)(2,1)S(1)} %get-tuple-element.4), channel_id=1, source_target_pairs={{0,1},{1,2},{2,3},{4,5},{5,6},{6,7},{8,9},{9,10},{10,11},{12,13},{... | collective-permute-start | bytes 221192 | tf_op jit(solution)/shard_map/ppermute | solution.py:12
  58.1 4.4 %collective-permute-start.3 = (bf16[18,1,16,128]{3,2,1,0:T(8,128)(2,1)S(1)}, bf16[18,1,16,128]{3,2,1,0:T(8,128)(2,1)S(1)}, u32[]{:S(2)}, u32[]{:S(2)}) collective-permute-start(bf16[18,1,16,128]{3,2,1,0:T(8,128)(2,1)S(1)} %get-tuple-element.5), channel_id=1, source_target_pairs={{1,0},{2,1},{3,2},{5,4},{6,5},{7,6},{9,8},{10,9},{11,10},{13,12},{... | collective-permute-start | bytes 221192 | tf_op jit(solution)/shard_map/ppermute | solution.py:15
  63.5 11.7 %copy-start.4 = (f32[8,16,128]{2,1,0:T(8,128)S(1)}, f32[8,16,128]{2,1,0:T(8,128)}, u32[]{:S(2)}) copy-start(f32[8,16,128]{2,1,0:T(8,128)} %param.8) | copy-start | bytes 196612
  63.5 11.7 %copy-start.6 = (s32[8,16]{1,0:T(8,128)S(1)}, s32[8,16]{1,0:T(8,128)}, u32[]{:S(2)}) copy-start(s32[8,16]{1,0:T(8,128)} %multiply_add_fusion) | copy-start | bytes 1540
  64.3 1.0 %copy-start.2 = (bf16[4096,128]{1,0:T(8,128)(2,1)}, bf16[4096,128]{1,0:T(8,128)(2,1)S(1)}, u32[]{:S(2)}) copy-start(bf16[4096,128]{1,0:T(8,128)(2,1)S(1)} %fusion.3) | copy-start | bytes 3145732
  66.9 8.4 %all-to-all-start.1 = ((bf16[4,64,128]{2,1,0:T(8,128)(2,1)}), bf16[4,64,128]{2,1,0:T(8,128)(2,1)S(1)}, u32[]{:S(2)}, u32[]{:S(2)}) async-start(bf16[4,64,128]{2,1,0:T(8,128)(2,1)} %bitcast.18), calls=%async_computation.1 | async-start | bytes 131072 | tf_op jit(solution)/shard_map/all_to_all | solution.py:67
where the time goes:
time: 77 us; the launch traced here: 76.1 us
  starting transfers between devices  39.2 us (51%)
  local copies, waits for them, and re-layouts  12.8 us (17%)
  waiting for transfers between devices  10.1 us (13%)
  other arithmetic  8.95 us (12%)
  matrix products  4.1 us (5%)
  between operations  0.92 us (1%)
    ppermute x6, starting transfers between devices, padded_2(): lax.ppermute(lax.slice_in_dim(block, block.shape[dim] - width, None, axis...  24 us
    ppermute x6, starting transfers between devices, padded_2(): lax.ppermute(lax.slice_in_dim(block, 0, width, axis=dim), axis, backward)  7.73 us
    ppermute x6, waiting for transfers between devices, padded_2(): lax.ppermute(lax.slice_in_dim(block, 0, width, axis=dim), axis, backward)  6.7 us
    all_to_all x1, starting transfers between devices, per_device(): lax.all_to_all(picked, 'gy', split_axis=0, concat_axis=0, tiled=True)  4.28 us
    all_to_all x1, waiting for transfers between devices, per_device(): lax.all_to_all(picked, 'gy', split_axis=0, concat_axis=0, tiled=True)  3.38 us
    dot_general x7, matrix products, couple(): jnp.dot(terms[index].reshape(-1, width), coupling[index], preferred_eleme...  3.25 us
    all_to_all x1, starting transfers between devices, per_device(): lax.all_to_all(nodes, 'gy', split_axis=0, concat_axis=0, tiled=True)  3.2 us
    unnamed x19, local copies, waits for them, and re-layouts  2.64 us
  transfers between devices with their start and end apart: 14, of which 4 were waited for; matrix products, arithmetic and copies ran while one was open for 28% of the time, Pallas kernels for 0%

commit v1 on v0

v1 whole, which is shorter than its diff:
```python
import functools

import jax
import jax.numpy as jnp
from jax import lax
from jax.experimental import pallas as pl
from jax.experimental.pallas import tpu as pltpu
from jax.sharding import PartitionSpec as P

MESH = pl.DeviceIdType.MESH
BF, F32 = jnp.bfloat16, jnp.float32


def kernel(
    nx, ny, early,
    x_hbm, c_hbm, lf_hbm, sc_hbm, live_hbm, tn_hbm,
    out_ref, grad_ref,
    px, cw, lf, sc, live, tn,
    stage, x0, edge, halo0,
    lf_edge, lf_halo, lf_corner, field, once,
    nodes_out, nodes_in, pick, picked, received,
    local_sem, h0_send, h0_recv, hx_send, hx_recv, lf_send, lf_recv, lc_send, lc_recv,
    nd_send, nd_recv, pk_send, pk_recv,
):
    i, j = lax.axis_index("gx"), lax.axis_index("gy")
    rows, cols, layers, width = x_hbm.shape
    faces = rows * cols
    slots = faces // ny
    tile_a, tile_b = once.shape[0] - 2, cols
    tile_nodes = tile_a * tile_b
    low_a, high_a, low_b, high_b = i > 0, i < nx - 1, j > 0, j < ny - 1
    one = lambda flag: flag.astype(jnp.int32)
    up = lambda v, n: lax.rem(v + 1, n)
    down = lambda v, n: lax.rem(v + n - 1, n)
    to = [(down(i, nx), j), (up(i, nx), j), (i, down(j, ny)), (i, up(j, ny))]
    has_to = [low_a, high_a, low_b, high_b]
    has_from = [high_a, low_a, high_b, low_b]
    corner_to = [(to[a][0], to[2 + b][1]) for a in (0, 1) for b in (0, 1)]
    corner_has_to = [has_to[a] & has_to[2 + b] for a in (0, 1) for b in (0, 1)]
    corner_has_from = [has_from[a] & has_from[2 + b] for a in (0, 1) for b in (0, 1)]

    loads = [
        pltpu.make_async_copy(src, dst, local_sem.at[n])
        for n, (src, dst) in enumerate(
            [
                (x_hbm, px.at[pl.ds(1, rows), pl.ds(1, cols)]),
                (lf_hbm, lf),
                (tn_hbm, tn),
                (live_hbm, live),
                (sc_hbm, sc),
                (c_hbm, cw),
            ]
        )
    ]
    for load in loads:
        load.start()

    barrier = pltpu.get_barrier_semaphore()
    for k in range(1, ny):
        pl.semaphore_signal(barrier, inc=1, device_id=(i, lax.rem(j + k, ny)), device_id_type=MESH)
    for flag, device in list(zip(has_to[:2], to[:2])) + list(zip(corner_has_to, corner_to)):

        @pl.when(flag)
        def _(device=device):
            pl.semaphore_signal(barrier, inc=1, device_id=device, device_id_type=MESH)

    partners = ny - 1 + (one(low_a) + one(high_a)) * (1 + one(low_b) + one(high_b))

    def zero_when(flag, ref, index):
        @pl.when(jnp.logical_not(flag))
        def _():
            ref[index] = jnp.zeros(ref.at[index].shape, ref.dtype)

    inner_a, inner_b = slice(1, rows + 1), slice(1, cols + 1)
    halo_at = [
        (rows + 1, inner_b),
        (0, inner_b),
        (inner_a, cols + 1),
        (inner_a, 0),
    ]
    for d in range(4):
        zero_when(has_from[d], px, halo_at[d])
        zero_when(has_from[d], halo0, d)
        zero_when(has_from[d], lf_halo, d)
        zero_when(corner_has_from[d], lf_corner, d)

    loads[0].wait()
    stage[...] = px[inner_a, inner_b].astype(F32)[:, :, 0:8, :].reshape(faces * 8, width)
    x0[inner_a, 8 : 8 + cols] = stage[pl.ds(0, faces, stride=8), :].reshape(rows, cols, width)
    edge[0] = x0[1, 8 : 8 + cols].astype(BF)
    edge[1] = x0[rows, 8 : 8 + cols].astype(BF)
    edge[2] = stage[pl.ds(0, rows, stride=8 * cols), :].astype(BF)
    edge[3] = stage[pl.ds(8 * (cols - 1), rows, stride=8 * cols), :].astype(BF)

    def remote(src, dst, send, recv, device):
        return pltpu.make_async_remote_copy(
            src_ref=src, dst_ref=dst, send_sem=send, recv_sem=recv, device_id=device, device_id_type=MESH
        )

    layer_copies = [
        remote(edge.at[d], halo0.at[d], h0_send.at[d], h0_recv.at[d], to[d]) for d in range(4)
    ]
    x_edges = [x_hbm.at[0], x_hbm.at[rows - 1], x_hbm.at[:, 0], x_hbm.at[:, cols - 1]]
    x_halos = [
        px.at[rows + 1, pl.ds(1, cols)],
        px.at[0, pl.ds(1, cols)],
        px.at[pl.ds(1, rows), cols + 1],
        px.at[pl.ds(1, rows), 0],
    ]
    x_copies = [
        remote(x_edges[d], x_halos[d], hx_send.at[d], hx_recv.at[d], to[d]) for d in range(4)
    ]
    two = 2 * tile_b
    lf_srcs = [lf.at[pl.ds(0, two)], lf.at[pl.ds(tile_nodes - two, two)], lf_edge.at[0], lf_edge.at[1]]
    lf_dsts = [lf_halo.at[0], lf_halo.at[1], lf_halo.at[2, pl.ds(0, 2 * tile_a)], lf_halo.at[3, pl.ds(0, 2 * tile_a)]]
    lf_copies = [
        remote(lf_srcs[d], lf_dsts[d], lf_send.at[d], lf_recv.at[d], to[d]) for d in range(4)
    ]
    corner_rows = [0, tile_b - 8, tile_nodes - tile_b, tile_nodes - 8]
    corner_copies = [
        remote(lf.at[pl.ds(corner_rows[d], 8)], lf_corner.at[d], lc_send.at[d], lc_recv.at[d], corner_to[d])
        for d in range(4)
    ]

    def start_when(flag, copy):
        @pl.when(flag)
        def _():
            copy.start()

    pl.semaphore_wait(barrier, partners)
    for d in range(4):
        start_when(has_to[d], layer_copies[d])
    for d in range(4):
        start_when(has_to[d], x_copies[d])

    loads[1].wait()
    loads[2].wait()
    loads[3].wait()
    slot_id = lax.broadcasted_iota(jnp.int32, (1, slots), 1)
    nodes_out[...] = jnp.full(nodes_out.shape, -1, jnp.int32)
    for o in range(ny):
        count = live[0:1, o : o + 1]
        nodes_out[o, 0:1, 0:slots] = jnp.where(slot_id < count, tn[o : o + 1, :], -1)

    def row_copies(src, dst, send, recv, per_owner):
        sends, receives = [], []
        for k in range(1, ny):
            target, source = lax.rem(j + k, ny), lax.rem(j + ny - k, ny)
            sends.append(
                remote(src(target), dst(j), send.at[k - 1], recv.at[k - 1], (i, target))
            )
            receives.append(
                remote(src(target), dst(source), send.at[k - 1], recv.at[k - 1], (i, target))
            )
        return sends, receives

    node_sends, node_receives = row_copies(
        lambda o: nodes_out.at[o], lambda o: nodes_in.at[o], nd_send, nd_recv, 1
    )
    for copy in node_sends:
        copy.start()
    nodes_in[j] = nodes_out[j]

    lf_edge[0, 0:tile_a] = lf[pl.ds(0, tile_a, stride=tile_b), :]
    lf_edge[0, tile_a : 2 * tile_a] = lf[pl.ds(1, tile_a, stride=tile_b), :]
    lf_edge[1, 0:tile_a] = lf[pl.ds(tile_b - 2, tile_a, stride=tile_b), :]
    lf_edge[1, tile_a : 2 * tile_a] = lf[pl.ds(tile_b - 1, tile_a, stride=tile_b), :]
    for d in range(4):
        start_when(has_to[d], lf_copies[d])
    for d in range(4):
        start_when(corner_has_to[d], corner_copies[d])

    loads[4].wait()
    column = jnp.broadcast_to(sc[0:1, :].astype(F32), (128, faces)).T
    for part in range(faces // 128):
        face_id = lax.broadcasted_iota(jnp.int32, (faces, 128), 1) + 128 * part
        pick[:, 128 * part : 128 * (part + 1)] = (column == face_id.astype(F32)).astype(BF)

    loads[5].wait()

    def product(a0, na, b0, nb):
        own = px[pl.ds(a0 + 1, na), b0 + 1 : b0 + 1 + nb]
        count = na * nb
        wide = own.astype(F32).reshape(count, layers, width)
        layer = lax.broadcasted_iota(jnp.int32, wide.shape, 1)
        below = jnp.where(layer == 0, 0.0, pltpu.roll(wide, 1, 1)).astype(BF)
        above = jnp.where(layer == layers - 1, 0.0, pltpu.roll(wide, layers - 1, 1)).astype(BF)
        flat = lambda v: v.reshape(count * layers, width)
        terms = [
            own,
            below,
            above,
            px[pl.ds(a0, na), b0 + 1 : b0 + 1 + nb],
            px[pl.ds(a0 + 2, na), b0 + 1 : b0 + 1 + nb],
            px[pl.ds(a0 + 1, na), b0 : b0 + nb],
            px[pl.ds(a0 + 1, na), b0 + 2 : b0 + 2 + nb],
        ]
        lhs = jnp.concatenate([flat(t) for t in terms], axis=1)
        total = jnp.dot(lhs, cw[...].reshape(7 * width, width), preferred_element_type=F32)
        out_ref[pl.ds(a0, na), b0 : b0 + nb] = total.astype(BF).reshape(na, nb, layers, width)

    def interior(first, last):
        def body(n, carry):
            product(1 + 2 * n, 2, 1, cols - 2)
            return carry

        lax.fori_loop(first, last, body, 0)

    interior(0, early)

    for d in range(4):
        pl.when(has_from[d])(layer_copies[d].wait_recv)
    x0[rows + 1, 8 : 8 + cols] = halo0[0].astype(F32)
    x0[0, 8 : 8 + cols] = halo0[1].astype(F32)
    x0[inner_a, 8 + cols : 9 + cols] = halo0[2].astype(F32).reshape(rows, 1, width)
    x0[inner_a, 7:8] = halo0[3].astype(F32).reshape(rows, 1, width)
    basal_terms = [
        x0[inner_a, 8 : 8 + cols].reshape(faces, width),
        stage[pl.ds(1, faces, stride=8), :],
        x0[0:rows, 8 : 8 + cols].reshape(faces, width),
        x0[2 : rows + 2, 8 : 8 + cols].reshape(faces, width),
        x0[inner_a, 7 : 7 + cols].reshape(faces, width),
        x0[inner_a, 9 : 9 + cols].reshape(faces, width),
    ]
    basal_lhs = jnp.concatenate([t.astype(BF) for t in basal_terms], axis=1)
    basal_w = jnp.concatenate([cw[0], cw[2:7].reshape(5 * width, width)], axis=0)
    basal = jnp.dot(basal_lhs, basal_w, preferred_element_type=F32).astype(BF)
    picked[...] = jnp.dot(pick[...], basal, preferred_element_type=F32).astype(BF)

    def slot_rows(ref):
        return lambda o: ref.at[pl.ds(pl.multiple_of(o * slots, slots), slots)]

    block_sends, block_receives = row_copies(
        slot_rows(picked), slot_rows(received), pk_send, pk_recv, slots
    )
    for copy in block_sends:
        copy.start()
    mine = pl.ds(pl.multiple_of(j * slots, slots), slots)
    received[mine, :] = picked[mine, :]

    interior(early, (rows - 2) // 2)

    for d in range(4):
        pl.when(has_from[d])(x_copies[d].wait_recv)
    product(0, 1, 0, cols)
    product(rows - 1, 1, 0, cols)
    product(1, rows - 2, 0, 1)
    product(1, rows - 2, cols - 1, 1)

    for d in range(4):
        pl.when(has_from[d])(lf_copies[d].wait_recv)
    for d in range(4):
        pl.when(corner_has_from[d])(corner_copies[d].wait_recv)
    field[...] = jnp.zeros_like(field)
    field[2 : 2 + tile_a, 8 : 8 + tile_b] = lf[...].reshape(tile_a, tile_b, width)
    field[2 + tile_a : 4 + tile_a, 8 : 8 + tile_b] = lf_halo[0].reshape(2, tile_b, width)
    field[0:2, 8 : 8 + tile_b] = lf_halo[1].reshape(2, tile_b, width)
    for side, at in ((2, 8 + tile_b), (3, 6)):
        for c in range(2):
            field[2 : 2 + tile_a, at + c : at + c + 1] = lf_halo[
                side, c * tile_a : (c + 1) * tile_a
            ].reshape(tile_a, 1, width)
    for d, (row, col, at) in enumerate(
        [(2 + tile_a, 8 + tile_b, 0), (2 + tile_a, 7, 7), (1, 8 + tile_b, 0), (1, 7, 7)]
    ):
        field[row, col : col + 1] = lf_corner[d, at : at + 1]

    def stencil(ref, a0, na, b0, nb):
        beside = (
            ref[a0 + 1 : a0 + 1 + na, b0 : b0 + nb]
            + ref[a0 - 1 : a0 - 1 + na, b0 : b0 + nb]
            + ref[a0 : a0 + na, b0 + 1 : b0 + 1 + nb]
            + ref[a0 : a0 + na, b0 - 1 : b0 - 1 + nb]
        )
        return 1.3 * ref[a0 : a0 + na, b0 : b0 + nb] - 0.2 * beside

    first = stencil(field, 1, tile_a + 2, 7, tile_b + 2)
    row_id = lax.broadcasted_iota(jnp.int32, first.shape, 0) + i * tile_a - 1
    col_id = lax.broadcasted_iota(jnp.int32, first.shape, 1) + j * tile_b - 1
    inside = (row_id >= 0) & (row_id < nx * tile_a) & (col_id >= 0) & (col_id < ny * tile_b)
    once[:, 7 : 9 + tile_b] = jnp.where(inside, first, 0.0)
    prior = stencil(once, 1, tile_a, 8, tile_b).reshape(tile_nodes, width)
    scale = jnp.exp(lf[...])

    for copy in node_receives:
        copy.wait_recv()
    node_id = lax.broadcasted_iota(jnp.int32, (tile_nodes, slots), 0)
    onehots = [(node_id == nodes_in[o, 0:1, 0:slots]).astype(F32).astype(BF) for o in range(ny)]
    for copy in block_receives:
        copy.wait_recv()
    misfit = jnp.zeros((tile_nodes, width), F32)
    for o in range(ny):
        misfit = misfit + jnp.dot(
            onehots[o], received[o * slots : (o + 1) * slots], preferred_element_type=F32
        )
    grad_ref[...] = scale * misfit + prior

    for d in range(4):
        pl.when(has_to[d])(layer_copies[d].wait_send)
        pl.when(has_to[d])(x_copies[d].wait_send)
        pl.when(has_to[d])(lf_copies[d].wait_send)
        pl.when(corner_has_to[d])(corner_copies[d].wait_send)
    for copy in node_sends + block_sends:
        copy.wait_send()


def solution(mesh):
    nx, ny = mesh.shape["gx"], mesh.shape["gy"]

    def per_device(adjoint_trace, coupling, log_friction, send_column, live_count, target_node):
        rows, cols, layers, width = adjoint_trace.shape
        tile_a, tile_b, _ = log_friction.shape
        tile_nodes = tile_a * tile_b
        faces = rows * cols
        slots = faces // ny
        vmem = pltpu.VMEM
        dma = pltpu.SemaphoreType.DMA
        anywhere = pl.BlockSpec(memory_space=pl.ANY)
        trace_update, gradient = pl.pallas_call(
            functools.partial(kernel, nx, ny, 3),
            out_shape=(
                jax.ShapeDtypeStruct(adjoint_trace.shape, BF),
                jax.ShapeDtypeStruct((tile_nodes, width), F32),
            ),
            in_specs=[anywhere] * 6,
            out_specs=(pl.BlockSpec(memory_space=vmem), pl.BlockSpec(memory_space=vmem)),
            scratch_shapes=[
                vmem((rows + 2, cols + 2, layers, width), BF),
                vmem(coupling.shape, BF),
                vmem((tile_nodes, width), F32),
                vmem((1, faces), jnp.int32),
                vmem((1, ny), jnp.int32),
                vmem((ny, slots), jnp.int32),
                vmem((faces * 8, width), F32),
                vmem((rows + 2, cols + 16, width), F32),
                vmem((4, 16, width), BF),
                vmem((4, 16, width), BF),
                vmem((2, 2 * tile_a, width), F32),
                vmem((4, 2 * tile_b, width), F32),
                vmem((4, 8, width), F32),
                vmem((tile_a + 4, tile_b + 16, width), F32),
                vmem((tile_a + 2, tile_b + 16, width), F32),
                vmem((ny, 8, 128), jnp.int32),
                vmem((ny, 8, 128), jnp.int32),
                vmem((faces, faces), BF),
                vmem((faces, width), BF),
                vmem((faces, width), BF),
                dma((6,)),
                *[dma((4,)) for _ in range(8)],
                *[dma((ny - 1,)) for _ in range(4)],
            ],
            compiler_params=pltpu.CompilerParams(
                collective_id=0, has_side_effects=True, vmem_limit_bytes=40 * 2**20
            ),
            cost_estimate=pl.CostEstimate(
                flops=2 * 7 * faces * layers * width * width,
                bytes_accessed=4 * faces * layers * width,
                transcendentals=tile_nodes * width,
            ),
        )(
            adjoint_trace,
            coupling,
            log_friction.reshape(tile_nodes, width),
            send_column.reshape(1, faces),
            live_count.reshape(1, ny),
            target_node.reshape(ny, slots),
        )
        return trace_update, gradient.reshape(tile_a, tile_b, width)

    in_specs = (
        P("gx", "gy", None, None),
        P(),
        P("gx", "gy", None),
        P("gx", "gy", None),
        P("gx", "gy", None),
        P("gx", "gy", None, None),
    )
    out_specs = (P("gx", "gy", None, None), P("gx", "gy", None))
    return jax.shard_map(
        per_device, mesh=mesh, in_specs=in_specs, out_specs=out_specs, check_vma=False
    )
```

time: 77 us -> 17.3 us (0.22)
  the two profiles are of different devices: /device:TPU:0 before, /device:TPU:9 now
where the time goes in v1:
time: 17.3 us; the launch traced here: 17.1 us
  Pallas kernels  11.1 us (64%)
  local copies, waits for them, and re-layouts  5.28 us (31%)
  between operations  0.67 us (4%)
    pallas_call x1, Pallas kernels, per_device(): pl.pallas_call(functools.partial(kernel, nx, ny, 3), out_shape=(jax.Shape...  11.1 us
    unnamed x14, local copies, waits for them, and re-layouts  5.28 us

profile of v1, /device:TPU:9, one launch (start us, length us, event | category | flops | bytes accessed | tf_op | source)
XLA Modules:
  0.0 17.1 jit_solution(11127128630724739980)
XLA Ops:
  0.6 0.0 copy-start.3
  0.6 0.0 copy-start.4
  0.7 0.0 copy-start.5
  0.7 0.7 %copy-done.3 = s32[1,1,4,64]{3,2,1,0:T(4,128)S(1)} copy-done((s32[1,1,4,64]{3,2,1,0:T(4,128)S(1)}, s32[1,1,4,64]{3,2,1,0:T(4,128)}, u32[]{:S(2)}) %copy-start.3) | copy-done | bytes 1048
  1.3 0.0 copy-done.4
  1.3 0.0 copy-done.5
  1.3 0.0 copy-start
  1.3 1.2 %copy-done = bf16[16,16,16,128]{3,2,1,0:T(8,128)(2,1)S(1)} copy-done((bf16[16,16,16,128]{3,2,1,0:T(8,128)(2,1)S(1)}, bf16[16,16,16,128]{3,2,1,0:T(8,128)(2,1)}, u32[]{:S(2)}) %copy-start) | copy-done | bytes 1048600
  2.6 0.0 copy-start.1
  2.6 0.9 %copy-done.1 = bf16[7,128,128]{2,1,0:T(8,128)(2,1)S(1)} copy-done((bf16[7,128,128]{2,1,0:T(8,128)(2,1)S(1)}, bf16[7,128,128]{2,1,0:T(8,128)(2,1)}, u32[]{:S(2)}) %copy-start.1) | copy-done | bytes 229400
  3.5 0.0 copy-start.2
  3.5 0.8 %copy-done.2 = f32[8,16,128]{2,1,0:T(8,128)S(1)} copy-done((f32[8,16,128]{2,1,0:T(8,128)S(1)}, f32[8,16,128]{2,1,0:T(8,128)}, u32[]{:S(2)}) %copy-start.2) | copy-done | bytes 65560
  4.3 11.1 %shard_map.77 = (bf16[16,16,16,128]{3,2,1,0:T(8,128)(2,1)S(1)}, f32[128,128]{1,0:T(8,128)S(1)}) custom-call(bf16[16,16,16,128]{3,2,1,0:T(8,128)(2,1)S(1)} %copy-done, bf16[7,128,128]{2,1,0:T(8,128)(2,1)S(1)} %copy-done.1, f32[128,128]{1,0:T(8,128)S(1)} %bitcast.6, s32[1,256]{1,0:T(1,128)S(1)} %bitcast.8, s32[1,4]{1,0:T(1,128)S(1)} %bitcast.9, ...), custom_call_target="tpu_custom_call" | custom-call | flops 939524096 | bytes 2097152 | tf_op jit(solution)/shard_map/pallas_call | solution.py:319
  15.5 1.0 %copy.10 = bf16[16,16,16,128]{3,2,1,0:T(8,128)(2,1)} copy(bf16[16,16,16,128]{3,2,1,0:T(8,128)(2,1)S(1)} %get-tuple-element.8) | data formatting | bytes 2097152
  16.4 0.6 %copy.11 = f32[8,16,128]{2,1,0:T(8,128)} copy(f32[8,16,128]{2,1,0:T(8,128)S(1)} %bitcast.5) | data formatting | bytes 131072
Async XLA Ops:
  0.6 0.7 %copy-start.3 = (s32[1,1,4,64]{3,2,1,0:T(4,128)S(1)}, s32[1,1,4,64]{3,2,1,0:T(4,128)}, u32[]{:S(2)}) copy-start(s32[1,1,4,64]{3,2,1,0:T(4,128)} %param.11) | copy-start | bytes 3076
  0.6 0.7 %copy-start.4 = (s32[1,1,256]{2,1,0:T(1,128)S(1)}, s32[1,1,256]{2,1,0:T(1,128)}, u32[]{:S(2)}) copy-start(s32[1,1,256]{2,1,0:T(1,128)} %param.9) | copy-start | bytes 3076
  0.7 0.7 %copy-start.5 = (s32[1,1,4]{2,1,0:T(1,128)S(1)}, s32[1,1,4]{2,1,0:T(1,128)}, u32[]{:S(2)}) copy-start(s32[1,1,4]{2,1,0:T(1,128)} %param.10) | copy-start | bytes 52
  1.3 1.2 %copy-start = (bf16[16,16,16,128]{3,2,1,0:T(8,128)(2,1)S(1)}, bf16[16,16,16,128]{3,2,1,0:T(8,128)(2,1)}, u32[]{:S(2)}) copy-start(bf16[16,16,16,128]{3,2,1,0:T(8,128)(2,1)} %x_hbm.1) | copy-start | bytes 3145732
  2.6 0.9 %copy-start.1 = (bf16[7,128,128]{2,1,0:T(8,128)(2,1)S(1)}, bf16[7,128,128]{2,1,0:T(8,128)(2,1)}, u32[]{:S(2)}) copy-start(bf16[7,128,128]{2,1,0:T(8,128)(2,1)} %c_hbm.1) | copy-start | bytes 688132
  3.5 0.8 %copy-start.2 = (f32[8,16,128]{2,1,0:T(8,128)S(1)}, f32[8,16,128]{2,1,0:T(8,128)}, u32[]{:S(2)}) copy-start(f32[8,16,128]{2,1,0:T(8,128)} %param.8) | copy-start | bytes 196612

commit v2 on v1

--- a/solution.py
+++ b/solution.py
@@ -11,14 +11,94 @@
 BF, F32 = jnp.bfloat16, jnp.float32
 
 
+def product(px, cw, out_ref, a0, na, b0, nb):
+    layers, width = px.shape[2:]
+    own = px[pl.ds(a0 + 1, na), b0 + 1 : b0 + 1 + nb]
+    count = na * nb
+    wide = own.astype(F32).reshape(count, layers, width)
+    layer = lax.broadcasted_iota(jnp.int32, wide.shape, 1)
+    below = jnp.where(layer == 0, 0.0, pltpu.roll(wide, 1, 1)).astype(BF)
+    above = jnp.where(layer == layers - 1, 0.0, pltpu.roll(wide, layers - 1, 1)).astype(BF)
+    flat = lambda v: v.reshape(count * layers, width)
+    terms = [
+        own,
+        below,
+        above,
+        px[pl.ds(a0, na), b0 + 1 : b0 + 1 + nb],
+        px[pl.ds(a0 + 2, na), b0 + 1 : b0 + 1 + nb],
+        px[pl.ds(a0 + 1, na), b0 : b0 + nb],
+        px[pl.ds(a0 + 1, na), b0 + 2 : b0 + 2 + nb],
+    ]
+    lhs = jnp.concatenate([flat(t) for t in terms], axis=1)
+    total = jnp.dot(lhs, cw[...].reshape(7 * width, width), preferred_element_type=F32)
+    out_ref[pl.ds(a0, na), b0 : b0 + nb] = total.astype(BF).reshape(na, nb, layers, width)
+
+
+def interior(px, cw, out_ref, first, last):
+    def body(n, carry):
+        product(px, cw, out_ref, 1 + 2 * n, 2, 1, px.shape[1] - 4)
+        return carry
+
+    if last > first:
+        lax.fori_loop(first, last, body, 0)
+
+
+def finish(
+    ny, late,
+    inner, px, cw, scale, prior, nodes, received,
+    out_hbm, grad_hbm,
+    rest, grad, sem,
+):
+    rows, cols = inner.shape[:2]
+    tile_nodes, width = scale.shape
+    slots = received.shape[0] // ny
+    done = 2 * late
+    writes = []
+
+    def write(src, dst):
+        copy = pltpu.make_async_copy(src, dst, sem.at[len(writes)])
+        copy.start()
+        writes.append(copy)
+
+    def write_part(ref, a0, na, b0, nb):
+        at = (pl.ds(a0, na), pl.ds(b0, nb))
+        write(ref.at[at], out_hbm.at[at])
+
+    write_part(inner, 1, done, 1, cols - 2)
+
+    node_id = lax.broadcasted_iota(jnp.int32, (tile_nodes, slots), 0)
+    misfit = jnp.zeros((tile_nodes, width), F32)
+    for o in range(ny):
+        onehot = (node_id == nodes[o, 0:1, 0:slots]).astype(F32).astype(BF)
+        misfit = misfit + jnp.dot(
+            onehot, received[o * slots : (o + 1) * slots], preferred_element_type=F32
+        )
+    grad[...] = scale[...] * misfit + prior[...]
+    write(grad, grad_hbm)
+
+    if done < rows - 2:
+        interior(px, cw, rest, late, (rows - 2) // 2)
+        write_part(rest, 1 + done, rows - 2 - done, 1, cols - 2)
+    for part in (
+        (0, 1, 0, cols),
+        (rows - 1, 1, 0, cols),
+        (1, rows - 2, 0, 1),
+        (1, rows - 2, cols - 1, 1),
+    ):
+        product(px, cw, rest, *part)
+        write_part(rest, *part)
+    for copy in writes:
+        copy.wait()
+
+
 def kernel(
-    nx, ny, early,
+    nx, ny, early, late,
     x_hbm, c_hbm, lf_hbm, sc_hbm, live_hbm, tn_hbm,
-    out_ref, grad_ref,
-    px, cw, lf, sc, live, tn,
+    out_ref, px, cw, scale, prior, nodes_in, received,
+    lf, sc, live, tn,
     stage, x0, edge, halo0,
     lf_edge, lf_halo, lf_corner, field, once,
-    nodes_out, nodes_in, pick, picked, received,
+    nodes_out, pick, picked,
     local_sem, h0_send, h0_recv, hx_send, hx_recv, lf_send, lf_recv, lc_send, lc_recv,
     nd_send, nd_recv, pk_send, pk_recv,
 ):
@@ -178,35 +258,7 @@
 
     loads[5].wait()
 
-    def product(a0, na, b0, nb):
-        own = px[pl.ds(a0 + 1, na), b0 + 1 : b0 + 1 + nb]
-        count = na * nb
-        wide = own.astype(F32).reshape(count, layers, width)
-        layer = lax.broadcasted_iota(jnp.int32, wide.shape, 1)
-        below = jnp.where(layer == 0, 0.0, pltpu.roll(wide, 1, 1)).astype(BF)
-        above = jnp.where(layer == layers - 1, 0.0, pltpu.roll(wide, layers - 1, 1)).astype(BF)
-        flat = lambda v: v.reshape(count * layers, width)
-        terms = [
-            own,
-            below,
-            above,
-            px[pl.ds(a0, na), b0 + 1 : b0 + 1 + nb],
-            px[pl.ds(a0 + 2, na), b0 + 1 : b0 + 1 + nb],
-            px[pl.ds(a0 + 1, na), b0 : b0 + nb],
-            px[pl.ds(a0 + 1, na), b0 + 2 : b0 + 2 + nb],
-        ]
-        lhs = jnp.concatenate([flat(t) for t in terms], axis=1)
-        total = jnp.dot(lhs, cw[...].reshape(7 * width, width), preferred_element_type=F32)
-        out_ref[pl.ds(a0, na), b0 : b0 + nb] = total.astype(BF).reshape(na, nb, layers, width)
-
-    def interior(first, last):
-        def body(n, carry):
-            product(1 + 2 * n, 2, 1, cols - 2)
-            return carry
-
-        lax.fori_loop(first, last, body, 0)
-
-    interior(0, early)
+    interior(px, cw, out_ref, 0, early)
 
     for d in range(4):
         pl.when(has_from[d])(layer_copies[d].wait_recv)
@@ -238,14 +290,7 @@
     mine = pl.ds(pl.multiple_of(j * slots, slots), slots)
     received[mine, :] = picked[mine, :]
 
-    interior(early, (rows - 2) // 2)
-
-    for d in range(4):
-        pl.when(has_from[d])(x_copies[d].wait_recv)
-    product(0, 1, 0, cols)
-    product(rows - 1, 1, 0, cols)
-    product(1, rows - 2, 0, 1)
-    product(1, rows - 2, cols - 1, 1)
+    interior(px, cw, out_ref, early, late)
 
     for d in range(4):
         pl.when(has_from[d])(lf_copies[d].wait_recv)
@@ -279,22 +324,13 @@
     col_id = lax.broadcasted_iota(jnp.int32, first.shape, 1) + j * tile_b - 1
     inside = (row_id >= 0) & (row_id < nx * tile_a) & (col_id >= 0) & (col_id < ny * tile_b)
     once[:, 7 : 9 + tile_b] = jnp.where(inside, first, 0.0)
-    prior = stencil(once, 1, tile_a, 8, tile_b).reshape(tile_nodes, width)
-    scale = jnp.exp(lf[...])
-
-    for copy in node_receives:
+    prior[...] = stencil(once, 1, tile_a, 8, tile_b).reshape(tile_nodes, width)
+    scale[...] = jnp.exp(lf[...])
+
+    for d in range(4):
+        pl.when(has_from[d])(x_copies[d].wait_recv)
+    for copy in node_receives + block_receives:
         copy.wait_recv()
-    node_id = lax.broadcasted_iota(jnp.int32, (tile_nodes, slots), 0)
-    onehots = [(node_id == nodes_in[o, 0:1, 0:slots]).astype(F32).astype(BF) for o in range(ny)]
-    for copy in block_receives:
-        copy.wait_recv()
-    misfit = jnp.zeros((tile_nodes, width), F32)
-    for o in range(ny):
-        misfit = misfit + jnp.dot(
-            onehots[o], received[o * slots : (o + 1) * slots], preferred_element_type=F32
-        )
-    grad_ref[...] = scale * misfit + prior
-
     for d in range(4):
         pl.when(has_to[d])(layer_copies[d].wait_send)
         pl.when(has_to[d])(x_copies[d].wait_send)
@@ -315,18 +351,24 @@
         slots = faces // ny
         vmem = pltpu.VMEM
         dma = pltpu.SemaphoreType.DMA
-        anywhere = pl.BlockSpec(memory_space=pl.ANY)
-        trace_update, gradient = pl.pallas_call(
-            functools.partial(kernel, nx, ny, 3),
+        hbm = pl.BlockSpec(memory_space=pltpu.HBM)
+        local = pl.BlockSpec(memory_space=vmem)
+        shape = jax.ShapeDtypeStruct
+        early, late = 3, (rows - 2) // 2
+        held = pl.pallas_call(
+            functools.partial(kernel, nx, ny, early, late),
             out_shape=(
-                jax.ShapeDtypeStruct(adjoint_trace.shape, BF),
-                jax.ShapeDtypeStruct((tile_nodes, width), F32),
+                shape(adjoint_trace.shape, BF),
+                shape((rows + 2, cols + 2, layers, width), BF),
+                shape(coupling.shape, BF),
+                shape((tile_nodes, width), F32),
+                shape((tile_nodes, width), F32),
+                shape((ny, 8, 128), jnp.int32),
+                shape((faces, width), BF),
             ),
-            in_specs=[anywhere] * 6,
-            out_specs=(pl.BlockSpec(memory_space=vmem), pl.BlockSpec(memory_space=vmem)),
+            in_specs=[hbm] * 6,
+            out_specs=(local,) * 7,
             scratch_shapes=[
-                vmem((rows + 2, cols + 2, layers, width), BF),
-                vmem(coupling.shape, BF),
                 vmem((tile_nodes, width), F32),
                 vmem((1, faces), jnp.int32),
                 vmem((1, ny), jnp.int32),
@@ -341,16 +383,14 @@
                 vmem((tile_a + 4, tile_b + 16, width), F32),
                 vmem((tile_a + 2, tile_b + 16, width), F32),
                 vmem((ny, 8, 128), jnp.int32),
-                vmem((ny, 8, 128), jnp.int32),
                 vmem((faces, faces), BF),
-                vmem((faces, width), BF),
                 vmem((faces, width), BF),
                 dma((6,)),
                 *[dma((4,)) for _ in range(8)],
                 *[dma((ny - 1,)) for _ in range(4)],
             ],
             compiler_params=pltpu.CompilerParams(
-                collective_id=0, has_side_effects=True, vmem_limit_bytes=40 * 2**20
+                collective_id=0, has_side_effects=True, vmem_limit_bytes=24 * 2**20
             ),
             cost_estimate=pl.CostEstimate(
                 flops=2 * 7 * faces * layers * width * width,
@@ -358,13 +398,30 @@
                 transcendentals=tile_nodes * width,
             ),
         )(
-            adjoint_trace,
-            coupling,
-            log_friction.reshape(tile_nodes, width),
-            send_column.reshape(1, faces),
-            live_count.reshape(1, ny),
-            target_node.reshape(ny, slots),
+            *[
+                pltpu.with_memory_space_constraint(operand, pltpu.HBM)
+                for operand in (
+                    adjoint_trace,
+                    coupling,
+                    log_friction.reshape(tile_nodes, width),
+                    send_column.reshape(1, faces),
+                    live_count.reshape(1, ny),
+                    target_node.reshape(ny, slots),
+                )
+            ]
         )
+        trace_update, gradient = pl.pallas_call(
+            functools.partial(finish, ny, late),
+            out_shape=(shape(adjoint_trace.shape, BF), shape((tile_nodes, width), F32)),
+            in_specs=[local] * 7,
+            out_specs=(hbm, hbm),
+            scratch_shapes=[
+                vmem(adjoint_trace.shape, BF),
+                vmem((tile_nodes, width), F32),
+                dma((8,)),
+            ],
+            compiler_params=pltpu.CompilerParams(vmem_limit_bytes=24 * 2**20),
+        )(*held)
         return trace_update, gradient.reshape(tile_a, tile_b, width)
 
     in_specs = (

time: 17.3 us -> 12.8 us (0.74)
  local copies, waits for them, and re-layouts: 5.28 us -> 0 us
  Pallas kernels: 11.1 us -> 12 us
    unnamed x14 -> x0, local copies, waits for them, and re-layouts: 5.28 us -> none
    pallas_call x1 -> x2, Pallas kernels: 11.1 us -> 12 us  [the longest x1 10.7 us: per_device(): pl.pallas_call(functools.partial(kernel, nx, ny, early, late), out_shape=...]
where the time goes in v2:
time: 12.8 us; the launch traced here: 12.6 us
  Pallas kernels  12 us (94%)
  between operations  0.64 us (5%)
    pallas_call x1, Pallas kernels, per_device(): pl.pallas_call(functools.partial(kernel, nx, ny, early, late), out_shape=...  10.7 us
    pallas_call x1, Pallas kernels, per_device(): pl.pallas_call(functools.partial(finish, ny, late), out_shape=(shape(adjo...  1.34 us

profile of v2, /device:TPU:9, one launch (start us, length us, event | category | flops | bytes accessed | tf_op | source)
XLA Modules:
  0.0 12.6 jit_solution(5614411125112776024)
XLA Ops:
  0.6 10.7 %shard_map.77 = (bf16[16,16,16,128]{3,2,1,0:T(8,128)(2,1)S(1)}, bf16[18,18,16,128]{3,2,1,0:T(8,128)(2,1)S(1)}, bf16[7,128,128]{2,1,0:T(8,128)(2,1)S(1)}, f32[128...) custom-call(bf16[16,16,16,128]{3,2,1,0:T(8,128)(2,1)} %x_hbm.1, ...), custom_call_target="tpu_custom_call" | custom-call | flops 939524096 | bytes 2097152 | tf_op jit(solution)/shard_map/pallas_call | solution.py:358
  11.3 1.3 %shard_map.78 = (bf16[16,16,16,128]{3,2,1,0:T(8,128)(2,1)}, f32[128,128]{1,0:T(8,128)}) custom-call(bf16[16,16,16,128]{3,2,1,0:T(8,128)(2,1)S(1)} %get-tuple-element.11.inner, bf16[18,18,16,128]{3,2,1,0:T(8,128)(2,1)S(1)} %get-tuple-element.12.px, bf16[7,128,128]{2,1,0:T(8,128)(2,1)S(1)} %get-tuple-element.13.cw, f32[128,128]{1,0:T(8,128)S(1)} %get-tuple-element.14.scale, ...), custom_call_target="tpu_custom_call" | custom-call | tf_op jit(solution)/shard_map/pallas_call | solution.py:413

commit v3 on v2

--- a/solution.py
+++ b/solution.py
@@ -132,9 +132,6 @@
             ]
         )
     ]
-    for load in loads:
-        load.start()
-
     barrier = pltpu.get_barrier_semaphore()
     for k in range(1, ny):
         pl.semaphore_signal(barrier, inc=1, device_id=(i, lax.rem(j + k, ny)), device_id_type=MESH)
@@ -143,6 +140,9 @@
         @pl.when(flag)
         def _(device=device):
             pl.semaphore_signal(barrier, inc=1, device_id=device, device_id_type=MESH)
+
+    for load in loads:
+        load.start()
 
     partners = ny - 1 + (one(low_a) + one(high_a)) * (1 + one(low_b) + one(high_b))
 
@@ -163,6 +163,30 @@
         zero_when(has_from[d], halo0, d)
         zero_when(has_from[d], lf_halo, d)
         zero_when(corner_has_from[d], lf_corner, d)
+
+    def remote(src, dst, send, recv, device):
+        return pltpu.make_async_remote_copy(
+            src_ref=src, dst_ref=dst, send_sem=send, recv_sem=recv, device_id=device, device_id_type=MESH
+        )
+
+    x_edges = [x_hbm.at[0], x_hbm.at[rows - 1], x_hbm.at[:, 0], x_hbm.at[:, cols - 1]]
+    x_halos = [
+        px.at[rows + 1, pl.ds(1, cols)],
+        px.at[0, pl.ds(1, cols)],
+        px.at[pl.ds(1, rows), cols + 1],
+        px.at[pl.ds(1, rows), 0],
+    ]
+    x_copies = [
+        remote(x_edges[d], x_halos[d], hx_send.at[d], hx_recv.at[d], to[d]) for d in range(4)
+    ]
+    def start_when(flag, copy):
+        @pl.when(flag)
+        def _():
+            copy.start()
+
+    pl.semaphore_wait(barrier, partners)
+    for d in range(4):
+        start_when(has_to[d], x_copies[d])
 
     loads[0].wait()
     stage[...] = px[inner_a, inner_b].astype(F32)[:, :, 0:8, :].reshape(faces * 8, width)
@@ -172,23 +196,8 @@
     edge[2] = stage[pl.ds(0, rows, stride=8 * cols), :].astype(BF)
     edge[3] = stage[pl.ds(8 * (cols - 1), rows, stride=8 * cols), :].astype(BF)
 
-    def remote(src, dst, send, recv, device):
-        return pltpu.make_async_remote_copy(
-            src_ref=src, dst_ref=dst, send_sem=send, recv_sem=recv, device_id=device, device_id_type=MESH
-        )
-
     layer_copies = [
         remote(edge.at[d], halo0.at[d], h0_send.at[d], h0_recv.at[d], to[d]) for d in range(4)
-    ]
-    x_edges = [x_hbm.at[0], x_hbm.at[rows - 1], x_hbm.at[:, 0], x_hbm.at[:, cols - 1]]
-    x_halos = [
-        px.at[rows + 1, pl.ds(1, cols)],
-        px.at[0, pl.ds(1, cols)],
-        px.at[pl.ds(1, rows), cols + 1],
-        px.at[pl.ds(1, rows), 0],
-    ]
-    x_copies = [
-        remote(x_edges[d], x_halos[d], hx_send.at[d], hx_recv.at[d], to[d]) for d in range(4)
     ]
     two = 2 * tile_b
     lf_srcs = [lf.at[pl.ds(0, two)], lf.at[pl.ds(tile_nodes - two, two)], lf_edge.at[0], lf_edge.at[1]]
@@ -202,16 +211,8 @@
         for d in range(4)
     ]
 
-    def start_when(flag, copy):
-        @pl.when(flag)
-        def _():
-            copy.start()
-
-    pl.semaphore_wait(barrier, partners)
     for d in range(4):
         start_when(has_to[d], layer_copies[d])
-    for d in range(4):
-        start_when(has_to[d], x_copies[d])
 
     loads[1].wait()
     loads[2].wait()

time: 12.8 us -> 14.3 us (1.12)
  Pallas kernels: 12 us -> 13.5 us
    pallas_call x1, Pallas kernels: 10.7 us -> 12.2 us  [per_device(): pl.pallas_call(functools.partial(kernel, nx, ny, early, late), out_shape=...]
where the time goes in v3:
time: 14.3 us; the launch traced here: 14.2 us
  Pallas kernels  13.5 us (94%)
  between operations  0.64 us (4%)
    pallas_call x1, Pallas kernels, per_device(): pl.pallas_call(functools.partial(kernel, nx, ny, early, late), out_shape=...  12.2 us
    pallas_call x1, Pallas kernels, per_device(): pl.pallas_call(functools.partial(finish, ny, late), out_shape=(shape(adjo...  1.34 us

profile of v3, /device:TPU:9, one launch (start us, length us, event | category | flops | bytes accessed | tf_op | source)
XLA Modules:
  0.0 14.2 jit_solution(3074827526122532045)
XLA Ops:
  0.6 12.2 %shard_map.77 = (bf16[16,16,16,128]{3,2,1,0:T(8,128)(2,1)S(1)}, bf16[18,18,16,128]{3,2,1,0:T(8,128)(2,1)S(1)}, bf16[7,128,128]{2,1,0:T(8,128)(2,1)S(1)}, f32[128...) custom-call(bf16[16,16,16,128]{3,2,1,0:T(8,128)(2,1)} %x_hbm.1, ...), custom_call_target="tpu_custom_call" | custom-call | flops 939524096 | bytes 2097152 | tf_op jit(solution)/shard_map/pallas_call | solution.py:359
  12.8 1.3 %shard_map.78 = (bf16[16,16,16,128]{3,2,1,0:T(8,128)(2,1)}, f32[128,128]{1,0:T(8,128)}) custom-call(bf16[16,16,16,128]{3,2,1,0:T(8,128)(2,1)S(1)} %get-tuple-element.11.inner, bf16[18,18,16,128]{3,2,1,0:T(8,128)(2,1)S(1)} %get-tuple-element.12.px, bf16[7,128,128]{2,1,0:T(8,128)(2,1)S(1)} %get-tuple-element.13.cw, f32[128,128]{1,0:T(8,128)S(1)} %get-tuple-element.14.scale, ...), custom_call_target="tpu_custom_call" | custom-call | tf_op jit(solution)/shard_map/pallas_call | solution.py:414

commit v4 on v2

--- a/solution.py
+++ b/solution.py
@@ -96,7 +96,7 @@
     x_hbm, c_hbm, lf_hbm, sc_hbm, live_hbm, tn_hbm,
     out_ref, px, cw, scale, prior, nodes_in, received,
     lf, sc, live, tn,
-    stage, x0, edge, halo0,
+    face, face_stage, stage, x0, edge, halo0,
     lf_edge, lf_halo, lf_corner, field, once,
     nodes_out, pick, picked,
     local_sem, h0_send, h0_recv, hx_send, hx_recv, lf_send, lf_recv, lc_send, lc_recv,
@@ -123,6 +123,10 @@
         pltpu.make_async_copy(src, dst, local_sem.at[n])
         for n, (src, dst) in enumerate(
             [
+                (x_hbm.at[0], face.at[0]),
+                (x_hbm.at[rows - 1], face.at[1]),
+                (x_hbm.at[:, 0], face.at[2]),
+                (x_hbm.at[:, cols - 1], face.at[3]),
                 (x_hbm, px.at[pl.ds(1, rows), pl.ds(1, cols)]),
                 (lf_hbm, lf),
                 (tn_hbm, tn),
@@ -132,8 +136,6 @@
             ]
         )
     ]
-    for load in loads:
-        load.start()
 
     barrier = pltpu.get_barrier_semaphore()
     for k in range(1, ny):
@@ -145,6 +147,9 @@
             pl.semaphore_signal(barrier, inc=1, device_id=device, device_id_type=MESH)
 
     partners = ny - 1 + (one(low_a) + one(high_a)) * (1 + one(low_b) + one(high_b))
+
+    for load in loads:
+        load.start()
 
     def zero_when(flag, ref, index):
         @pl.when(jnp.logical_not(flag))
@@ -164,13 +169,11 @@
         zero_when(has_from[d], lf_halo, d)
         zero_when(corner_has_from[d], lf_corner, d)
 
-    loads[0].wait()
-    stage[...] = px[inner_a, inner_b].astype(F32)[:, :, 0:8, :].reshape(faces * 8, width)
-    x0[inner_a, 8 : 8 + cols] = stage[pl.ds(0, faces, stride=8), :].reshape(rows, cols, width)
-    edge[0] = x0[1, 8 : 8 + cols].astype(BF)
-    edge[1] = x0[rows, 8 : 8 + cols].astype(BF)
-    edge[2] = stage[pl.ds(0, rows, stride=8 * cols), :].astype(BF)
-    edge[3] = stage[pl.ds(8 * (cols - 1), rows, stride=8 * cols), :].astype(BF)
+    for d in range(4):
+        loads[d].wait()
+    face_stage[...] = face[...].astype(F32)[:, :, 0:8, :].reshape(face_stage.shape)
+    for d in range(4):
+        edge[d] = face_stage[pl.ds(8 * rows * d, rows, stride=8), :].astype(BF)
 
     def remote(src, dst, send, recv, device):
         return pltpu.make_async_remote_copy(
@@ -213,9 +216,9 @@
     for d in range(4):
         start_when(has_to[d], x_copies[d])
 
-    loads[1].wait()
-    loads[2].wait()
-    loads[3].wait()
+    loads[5].wait()
+    loads[6].wait()
+    loads[7].wait()
     slot_id = lax.broadcasted_iota(jnp.int32, (1, slots), 1)
     nodes_out[...] = jnp.full(nodes_out.shape, -1, jnp.int32)
     for o in range(ny):
@@ -251,12 +254,16 @@
         start_when(corner_has_to[d], corner_copies[d])
 
     loads[4].wait()
+    stage[...] = px[inner_a, inner_b].astype(F32)[:, :, 0:8, :].reshape(faces * 8, width)
+    x0[inner_a, 8 : 8 + cols] = stage[pl.ds(0, faces, stride=8), :].reshape(rows, cols, width)
+
+    loads[8].wait()
     column = jnp.broadcast_to(sc[0:1, :].astype(F32), (128, faces)).T
     for part in range(faces // 128):
         face_id = lax.broadcasted_iota(jnp.int32, (faces, 128), 1) + 128 * part
         pick[:, 128 * part : 128 * (part + 1)] = (column == face_id.astype(F32)).astype(BF)
 
-    loads[5].wait()
+    loads[9].wait()
 
     interior(px, cw, out_ref, 0, early)
 
@@ -354,7 +361,7 @@
         hbm = pl.BlockSpec(memory_space=pltpu.HBM)
         local = pl.BlockSpec(memory_space=vmem)
         shape = jax.ShapeDtypeStruct
-        early, late = 3, (rows - 2) // 2
+        early, late = 0, (rows - 2) // 2
         held = pl.pallas_call(
             functools.partial(kernel, nx, ny, early, late),
             out_shape=(
@@ -373,6 +380,8 @@
                 vmem((1, faces), jnp.int32),
                 vmem((1, ny), jnp.int32),
                 vmem((ny, slots), jnp.int32),
+                vmem((4, rows, layers, width), BF),
+                vmem((4 * rows * 8, width), F32),
                 vmem((faces * 8, width), F32),
                 vmem((rows + 2, cols + 16, width), F32),
                 vmem((4, 16, width), BF),
@@ -385,7 +394,7 @@
                 vmem((ny, 8, 128), jnp.int32),
                 vmem((faces, faces), BF),
                 vmem((faces, width), BF),
-                dma((6,)),
+                dma((10,)),
                 *[dma((4,)) for _ in range(8)],
                 *[dma((ny - 1,)) for _ in range(4)],
             ],

time: 12.8 us -> 12.8 us (level)
  no operation moved by 1% of the time
where the time goes in v4:
time: 12.8 us; the launch traced here: 12.7 us
  Pallas kernels  12 us (94%)
  between operations  0.64 us (5%)
    pallas_call x1, Pallas kernels, per_device(): pl.pallas_call(functools.partial(kernel, nx, ny, early, late), out_shape=...  10.7 us
    pallas_call x1, Pallas kernels, per_device(): pl.pallas_call(functools.partial(finish, ny, late), out_shape=(shape(adjo...  1.34 us

profile of v4, /device:TPU:9, one launch (start us, length us, event | category | flops | bytes accessed | tf_op | source)
XLA Modules:
  0.0 12.7 jit_solution(592756234784216267)
XLA Ops:
  0.6 10.7 %shard_map.77 = (bf16[16,16,16,128]{3,2,1,0:T(8,128)(2,1)S(1)}, bf16[18,18,16,128]{3,2,1,0:T(8,128)(2,1)S(1)}, bf16[7,128,128]{2,1,0:T(8,128)(2,1)S(1)}, f32[128...) custom-call(bf16[16,16,16,128]{3,2,1,0:T(8,128)(2,1)} %x_hbm.1, ...), custom_call_target="tpu_custom_call" | custom-call | flops 939524096 | bytes 2097152 | tf_op jit(solution)/shard_map/pallas_call | solution.py:365
  11.3 1.3 %shard_map.78 = (bf16[16,16,16,128]{3,2,1,0:T(8,128)(2,1)}, f32[128,128]{1,0:T(8,128)}) custom-call(bf16[16,16,16,128]{3,2,1,0:T(8,128)(2,1)S(1)} %get-tuple-element.11.inner, bf16[18,18,16,128]{3,2,1,0:T(8,128)(2,1)S(1)} %get-tuple-element.12.px, bf16[7,128,128]{2,1,0:T(8,128)(2,1)S(1)} %get-tuple-element.13.cw, f32[128,128]{1,0:T(8,128)S(1)} %get-tuple-element.14.scale, ...), custom_call_target="tpu_custom_call" | custom-call | tf_op jit(solution)/shard_map/pallas_call | solution.py:422

commit v5 on v4

--- a/solution.py
+++ b/solution.py
@@ -34,17 +34,12 @@
     out_ref[pl.ds(a0, na), b0 : b0 + nb] = total.astype(BF).reshape(na, nb, layers, width)
 
 
-def interior(px, cw, out_ref, first, last):
-    def body(n, carry):
-        product(px, cw, out_ref, 1 + 2 * n, 2, 1, px.shape[1] - 4)
-        return carry
-
-    if last > first:
-        lax.fori_loop(first, last, body, 0)
+def interior(px, cw, out_ref, first, count):
+    product(px, cw, out_ref, first, count, 1, px.shape[1] - 4)
 
 
 def finish(
-    ny, late,
+    ny,
     inner, px, cw, scale, prior, nodes, received,
     out_hbm, grad_hbm,
     rest, grad, sem,
@@ -52,7 +47,6 @@
     rows, cols = inner.shape[:2]
     tile_nodes, width = scale.shape
     slots = received.shape[0] // ny
-    done = 2 * late
     writes = []
 
     def write(src, dst):
@@ -64,7 +58,7 @@
         at = (pl.ds(a0, na), pl.ds(b0, nb))
         write(ref.at[at], out_hbm.at[at])
 
-    write_part(inner, 1, done, 1, cols - 2)
+    write_part(inner, 1, rows - 2, 1, cols - 2)
 
     node_id = lax.broadcasted_iota(jnp.int32, (tile_nodes, slots), 0)
     misfit = jnp.zeros((tile_nodes, width), F32)
@@ -76,9 +70,6 @@
     grad[...] = scale[...] * misfit + prior[...]
     write(grad, grad_hbm)
 
-    if done < rows - 2:
-        interior(px, cw, rest, late, (rows - 2) // 2)
-        write_part(rest, 1 + done, rows - 2 - done, 1, cols - 2)
     for part in (
         (0, 1, 0, cols),
         (rows - 1, 1, 0, cols),
@@ -92,7 +83,7 @@
 
 
 def kernel(
-    nx, ny, early, late,
+    nx, ny,
     x_hbm, c_hbm, lf_hbm, sc_hbm, live_hbm, tn_hbm,
     out_ref, px, cw, scale, prior, nodes_in, received,
     lf, sc, live, tn,
@@ -165,9 +156,8 @@
     ]
     for d in range(4):
         zero_when(has_from[d], px, halo_at[d])
-        zero_when(has_from[d], halo0, d)
-        zero_when(has_from[d], lf_halo, d)
-        zero_when(corner_has_from[d], lf_corner, d)
+    x0[...] = jnp.zeros_like(x0)
+    field[...] = jnp.zeros_like(field)
 
     for d in range(4):
         loads[d].wait()
@@ -265,14 +255,17 @@
 
     loads[9].wait()
 
-    interior(px, cw, out_ref, 0, early)
-
-    for d in range(4):
-        pl.when(has_from[d])(layer_copies[d].wait_recv)
-    x0[rows + 1, 8 : 8 + cols] = halo0[0].astype(F32)
-    x0[0, 8 : 8 + cols] = halo0[1].astype(F32)
-    x0[inner_a, 8 + cols : 9 + cols] = halo0[2].astype(F32).reshape(rows, 1, width)
-    x0[inner_a, 7:8] = halo0[3].astype(F32).reshape(rows, 1, width)
+    def basal_halo(d):
+        layer_copies[d].wait_recv()
+        block = halo0[d].astype(F32)
+        if d < 2:
+            x0[(rows + 1, 0)[d], 8 : 8 + cols] = block
+        else:
+            at = (8 + cols, 7)[d - 2]
+            x0[inner_a, at : at + 1] = block.reshape(rows, 1, width)
+
+    for d in range(4):
+        pl.when(has_from[d])(functools.partial(basal_halo, d))
     basal_terms = [
         x0[inner_a, 8 : 8 + cols].reshape(faces, width),
         stage[pl.ds(1, faces, stride=8), :],
@@ -297,25 +290,34 @@
     mine = pl.ds(pl.multiple_of(j * slots, slots), slots)
     received[mine, :] = picked[mine, :]
 
-    interior(px, cw, out_ref, early, late)
-
-    for d in range(4):
-        pl.when(has_from[d])(lf_copies[d].wait_recv)
-    for d in range(4):
-        pl.when(corner_has_from[d])(corner_copies[d].wait_recv)
-    field[...] = jnp.zeros_like(field)
+    half = (rows - 2) // 2
+    interior(px, cw, out_ref, 1, half)
+    interior(px, cw, out_ref, 1 + half, rows - 2 - half)
+
     field[2 : 2 + tile_a, 8 : 8 + tile_b] = lf[...].reshape(tile_a, tile_b, width)
-    field[2 + tile_a : 4 + tile_a, 8 : 8 + tile_b] = lf_halo[0].reshape(2, tile_b, width)
-    field[0:2, 8 : 8 + tile_b] = lf_halo[1].reshape(2, tile_b, width)
-    for side, at in ((2, 8 + tile_b), (3, 6)):
-        for c in range(2):
-            field[2 : 2 + tile_a, at + c : at + c + 1] = lf_halo[
-                side, c * tile_a : (c + 1) * tile_a
-            ].reshape(tile_a, 1, width)
-    for d, (row, col, at) in enumerate(
-        [(2 + tile_a, 8 + tile_b, 0), (2 + tile_a, 7, 7), (1, 8 + tile_b, 0), (1, 7, 7)]
-    ):
-        field[row, col : col + 1] = lf_corner[d, at : at + 1]
+
+    def field_halo(d):
+        lf_copies[d].wait_recv()
+        if d < 2:
+            at = (2 + tile_a, 0)[d]
+            field[at : at + 2, 8 : 8 + tile_b] = lf_halo[d].reshape(2, tile_b, width)
+        else:
+            at = (8 + tile_b, 6)[d - 2]
+            for c in range(2):
+                field[2 : 2 + tile_a, at + c : at + c + 1] = lf_halo[
+                    d, c * tile_a : (c + 1) * tile_a
+                ].reshape(tile_a, 1, width)
+
+    def field_corner(d):
+        corner_copies[d].wait_recv()
+        row, at = (2 + tile_a, 1)[d // 2], (8 + tile_b, 7)[d % 2]
+        source = (0, 7)[d % 2]
+        field[row, at : at + 1] = lf_corner[d, source : source + 1]
+
+    for d in range(4):
+        pl.when(has_from[d])(functools.partial(field_halo, d))
+    for d in range(4):
+        pl.when(corner_has_from[d])(functools.partial(field_corner, d))
 
     def stencil(ref, a0, na, b0, nb):
         beside = (
@@ -338,10 +340,13 @@
         pl.when(has_from[d])(x_copies[d].wait_recv)
     for copy in node_receives + block_receives:
         copy.wait_recv()
-    for d in range(4):
-        pl.when(has_to[d])(layer_copies[d].wait_send)
-        pl.when(has_to[d])(x_copies[d].wait_send)
-        pl.when(has_to[d])(lf_copies[d].wait_send)
+    def sent(d):
+        layer_copies[d].wait_send()
+        x_copies[d].wait_send()
+        lf_copies[d].wait_send()
+
+    for d in range(4):
+        pl.when(has_to[d])(functools.partial(sent, d))
         pl.when(corner_has_to[d])(corner_copies[d].wait_send)
     for copy in node_sends + block_sends:
         copy.wait_send()
@@ -361,9 +366,8 @@
         hbm = pl.BlockSpec(memory_space=pltpu.HBM)
         local = pl.BlockSpec(memory_space=vmem)
         shape = jax.ShapeDtypeStruct
-        early, late = 0, (rows - 2) // 2
         held = pl.pallas_call(
-            functools.partial(kernel, nx, ny, early, late),
+            functools.partial(kernel, nx, ny),
             out_shape=(
                 shape(adjoint_trace.shape, BF),
                 shape((rows + 2, cols + 2, layers, width), BF),
@@ -420,7 +424,7 @@
             ]
         )
         trace_update, gradient = pl.pallas_call(
-            functools.partial(finish, ny, late),
+            functools.partial(finish, ny),
             out_shape=(shape(adjoint_trace.shape, BF), shape((tile_nodes, width), F32)),
             in_specs=[local] * 7,
             out_specs=(hbm, hbm),

time: 12.8 us -> 12.8 us (level)
  no operation moved by 1% of the time
where the time goes in v5:
time: 12.8 us; the launch traced here: 12.7 us
  Pallas kernels  12.1 us (95%)
  between operations  0.64 us (5%)
    pallas_call x1, Pallas kernels, per_device(): pl.pallas_call(functools.partial(kernel, nx, ny), out_shape=(shape(adjoin...  10.7 us
    pallas_call x1, Pallas kernels, per_device(): pl.pallas_call(functools.partial(finish, ny), out_shape=(shape(adjoint_tr...  1.34 us

profile of v5, /device:TPU:9, one launch (start us, length us, event | category | flops | bytes accessed | tf_op | source)
XLA Modules:
  0.0 12.7 jit_solution(1304184225012344223)
XLA Ops:
  0.6 10.7 %shard_map.77 = (bf16[16,16,16,128]{3,2,1,0:T(8,128)(2,1)S(1)}, bf16[18,18,16,128]{3,2,1,0:T(8,128)(2,1)S(1)}, bf16[7,128,128]{2,1,0:T(8,128)(2,1)S(1)}, f32[128...) custom-call(bf16[16,16,16,128]{3,2,1,0:T(8,128)(2,1)} %x_hbm.1, ...), custom_call_target="tpu_custom_call" | custom-call | flops 939524096 | bytes 2097152 | tf_op jit(solution)/shard_map/pallas_call | solution.py:369
  11.4 1.3 %shard_map.78 = (bf16[16,16,16,128]{3,2,1,0:T(8,128)(2,1)}, f32[128,128]{1,0:T(8,128)}) custom-call(bf16[16,16,16,128]{3,2,1,0:T(8,128)(2,1)S(1)} %get-tuple-element.11.inner, bf16[18,18,16,128]{3,2,1,0:T(8,128)(2,1)S(1)} %get-tuple-element.12.px, bf16[7,128,128]{2,1,0:T(8,128)(2,1)S(1)} %get-tuple-element.13.cw, f32[128,128]{1,0:T(8,128)S(1)} %get-tuple-element.14.scale, ...), custom_call_target="tpu_custom_call" | custom-call | tf_op jit(solution)/shard_map/pallas_call | solution.py:426

commit v6 on v5

--- a/solution.py
+++ b/solution.py
@@ -88,7 +88,7 @@
     out_ref, px, cw, scale, prior, nodes_in, received,
     lf, sc, live, tn,
     face, face_stage, stage, x0, edge, halo0,
-    lf_edge, lf_halo, lf_corner, field, once,
+    lf_stage, lf_edge, lf_halo, lf_corner, field, once,
     nodes_out, pick, picked,
     local_sem, h0_send, h0_recv, hx_send, hx_recv, lf_send, lf_recv, lc_send, lc_recv,
     nd_send, nd_recv, pk_send, pk_recv,
@@ -184,7 +184,7 @@
         remote(x_edges[d], x_halos[d], hx_send.at[d], hx_recv.at[d], to[d]) for d in range(4)
     ]
     two = 2 * tile_b
-    lf_srcs = [lf.at[pl.ds(0, two)], lf.at[pl.ds(tile_nodes - two, two)], lf_edge.at[0], lf_edge.at[1]]
+    lf_srcs = [lf_edge.at[0], lf_edge.at[1], lf_edge.at[2, pl.ds(0, 2 * tile_a)], lf_edge.at[3, pl.ds(0, 2 * tile_a)]]
     lf_dsts = [lf_halo.at[0], lf_halo.at[1], lf_halo.at[2, pl.ds(0, 2 * tile_a)], lf_halo.at[3, pl.ds(0, 2 * tile_a)]]
     lf_copies = [
         remote(lf_srcs[d], lf_dsts[d], lf_send.at[d], lf_recv.at[d], to[d]) for d in range(4)
@@ -203,7 +203,7 @@
     pl.semaphore_wait(barrier, partners)
     for d in range(4):
         start_when(has_to[d], layer_copies[d])
-    for d in range(4):
+    for d in range(2):
         start_when(has_to[d], x_copies[d])
 
     loads[5].wait()
@@ -230,18 +230,14 @@
     node_sends, node_receives = row_copies(
         lambda o: nodes_out.at[o], lambda o: nodes_in.at[o], nd_send, nd_recv, 1
     )
-    for copy in node_sends:
-        copy.start()
     nodes_in[j] = nodes_out[j]
 
-    lf_edge[0, 0:tile_a] = lf[pl.ds(0, tile_a, stride=tile_b), :]
-    lf_edge[0, tile_a : 2 * tile_a] = lf[pl.ds(1, tile_a, stride=tile_b), :]
-    lf_edge[1, 0:tile_a] = lf[pl.ds(tile_b - 2, tile_a, stride=tile_b), :]
-    lf_edge[1, tile_a : 2 * tile_a] = lf[pl.ds(tile_b - 1, tile_a, stride=tile_b), :]
-    for d in range(4):
-        start_when(has_to[d], lf_copies[d])
-    for d in range(4):
-        start_when(corner_has_to[d], corner_copies[d])
+    lf_edge[0] = lf[0:two].astype(BF)
+    lf_edge[1] = lf[tile_nodes - two : tile_nodes].astype(BF)
+    for d, first in ((2, 0), (3, tile_b - 2)):
+        for c in range(2):
+            lf_stage[c * tile_a : (c + 1) * tile_a] = lf[pl.ds(first + c, tile_a, stride=tile_b), :]
+        lf_edge[d, 0 : 2 * tile_a] = lf_stage[...].astype(BF)
 
     loads[4].wait()
     stage[...] = px[inner_a, inner_b].astype(F32)[:, :, 0:8, :].reshape(faces * 8, width)
@@ -287,6 +283,14 @@
     )
     for copy in block_sends:
         copy.start()
+    for copy in node_sends:
+        copy.start()
+    for d in range(4):
+        start_when(has_to[d], lf_copies[d])
+    for d in range(4):
+        start_when(corner_has_to[d], corner_copies[d])
+    for d in range(2, 4):
+        start_when(has_to[d], x_copies[d])
     mine = pl.ds(pl.multiple_of(j * slots, slots), slots)
     received[mine, :] = picked[mine, :]
 
@@ -300,12 +304,13 @@
         lf_copies[d].wait_recv()
         if d < 2:
             at = (2 + tile_a, 0)[d]
-            field[at : at + 2, 8 : 8 + tile_b] = lf_halo[d].reshape(2, tile_b, width)
+            field[at : at + 2, 8 : 8 + tile_b] = lf_halo[d].astype(F32).reshape(2, tile_b, width)
         else:
             at = (8 + tile_b, 6)[d - 2]
+            block = lf_halo[d, 0 : 2 * tile_a].astype(F32)
             for c in range(2):
-                field[2 : 2 + tile_a, at + c : at + c + 1] = lf_halo[
-                    d, c * tile_a : (c + 1) * tile_a
+                field[2 : 2 + tile_a, at + c : at + c + 1] = block[
+                    c * tile_a : (c + 1) * tile_a
                 ].reshape(tile_a, 1, width)
 
     def field_corner(d):
@@ -390,8 +395,9 @@
                 vmem((rows + 2, cols + 16, width), F32),
                 vmem((4, 16, width), BF),
                 vmem((4, 16, width), BF),
-                vmem((2, 2 * tile_a, width), F32),
-                vmem((4, 2 * tile_b, width), F32),
+                vmem((2 * tile_a, width), F32),
+                vmem((4, 2 * tile_b, width), BF),
+                vmem((4, 2 * tile_b, width), BF),
                 vmem((4, 8, width), F32),
                 vmem((tile_a + 4, tile_b + 16, width), F32),
                 vmem((tile_a + 2, tile_b + 16, width), F32),

time: 12.8 us -> 13.3 us (1.039)
  the two profiles are of different devices: /device:TPU:9 before, /device:TPU:1 now
where the time goes in v6:
time: 13.3 us; the launch traced here: 13.2 us
  Pallas kernels  12.5 us (94%)
  between operations  0.64 us (5%)
    pallas_call x1, Pallas kernels, per_device(): pl.pallas_call(functools.partial(kernel, nx, ny), out_shape=(shape(adjoin...  11.2 us
    pallas_call x1, Pallas kernels, per_device(): pl.pallas_call(functools.partial(finish, ny), out_shape=(shape(adjoint_tr...  1.34 us

profile of v6, /device:TPU:1, one launch (start us, length us, event | category | flops | bytes accessed | tf_op | source)
XLA Modules:
  0.0 13.2 jit_solution(11836060872791027696)
XLA Ops:
  0.6 11.2 %shard_map.77 = (bf16[16,16,16,128]{3,2,1,0:T(8,128)(2,1)S(1)}, bf16[18,18,16,128]{3,2,1,0:T(8,128)(2,1)S(1)}, bf16[7,128,128]{2,1,0:T(8,128)(2,1)S(1)}, f32[128...) custom-call(bf16[16,16,16,128]{3,2,1,0:T(8,128)(2,1)} %x_hbm.1, ...), custom_call_target="tpu_custom_call" | custom-call | flops 939524096 | bytes 2097152 | tf_op jit(solution)/shard_map/pallas_call | solution.py:374
  11.8 1.3 %shard_map.78 = (bf16[16,16,16,128]{3,2,1,0:T(8,128)(2,1)}, f32[128,128]{1,0:T(8,128)}) custom-call(bf16[16,16,16,128]{3,2,1,0:T(8,128)(2,1)S(1)} %get-tuple-element.11.inner, bf16[18,18,16,128]{3,2,1,0:T(8,128)(2,1)S(1)} %get-tuple-element.12.px, bf16[7,128,128]{2,1,0:T(8,128)(2,1)S(1)} %get-tuple-element.13.cw, f32[128,128]{1,0:T(8,128)S(1)} %get-tuple-element.14.scale, ...), custom_call_target="tpu_custom_call" | custom-call | tf_op jit(solution)/shard_map/pallas_call | solution.py:432

commit v7 on v6

--- a/solution.py
+++ b/solution.py
@@ -203,7 +203,7 @@
     pl.semaphore_wait(barrier, partners)
     for d in range(4):
         start_when(has_to[d], layer_copies[d])
-    for d in range(2):
+    for d in range(4):
         start_when(has_to[d], x_copies[d])
 
     loads[5].wait()
@@ -239,6 +239,13 @@
             lf_stage[c * tile_a : (c + 1) * tile_a] = lf[pl.ds(first + c, tile_a, stride=tile_b), :]
         lf_edge[d, 0 : 2 * tile_a] = lf_stage[...].astype(BF)
 
+    for copy in node_sends:
+        copy.start()
+    for d in range(4):
+        start_when(has_to[d], lf_copies[d])
+    for d in range(4):
+        start_when(corner_has_to[d], corner_copies[d])
+
     loads[4].wait()
     stage[...] = px[inner_a, inner_b].astype(F32)[:, :, 0:8, :].reshape(faces * 8, width)
     x0[inner_a, 8 : 8 + cols] = stage[pl.ds(0, faces, stride=8), :].reshape(rows, cols, width)
@@ -250,6 +257,9 @@
         pick[:, 128 * part : 128 * (part + 1)] = (column == face_id.astype(F32)).astype(BF)
 
     loads[9].wait()
+
+    half = (rows - 2) // 2
+    interior(px, cw, out_ref, 1, half)
 
     def basal_halo(d):
         layer_copies[d].wait_recv()
@@ -283,19 +293,9 @@
     )
     for copy in block_sends:
         copy.start()
-    for copy in node_sends:
-        copy.start()
-    for d in range(4):
-        start_when(has_to[d], lf_copies[d])
-    for d in range(4):
-        start_when(corner_has_to[d], corner_copies[d])
-    for d in range(2, 4):
-        start_when(has_to[d], x_copies[d])
     mine = pl.ds(pl.multiple_of(j * slots, slots), slots)
     received[mine, :] = picked[mine, :]
 
-    half = (rows - 2) // 2
-    interior(px, cw, out_ref, 1, half)
     interior(px, cw, out_ref, 1 + half, rows - 2 - half)
 
     field[2 : 2 + tile_a, 8 : 8 + tile_b] = lf[...].reshape(tile_a, tile_b, width)

time: 13.3 us -> 12.7 us (0.955)
  the two profiles are of different devices: /device:TPU:1 before, /device:TPU:9 now
where the time goes in v7:
time: 12.7 us; the launch traced here: 12.5 us
  Pallas kernels  11.9 us (94%)
  between operations  0.64 us (5%)
    pallas_call x1, Pallas kernels, per_device(): pl.pallas_call(functools.partial(kernel, nx, ny), out_shape=(shape(adjoin...  10.6 us
    pallas_call x1, Pallas kernels, per_device(): pl.pallas_call(functools.partial(finish, ny), out_shape=(shape(adjoint_tr...  1.34 us

profile of v7, /device:TPU:9, one launch (start us, length us, event | category | flops | bytes accessed | tf_op | source)
XLA Modules:
  0.0 12.5 jit_solution(18381083326039829779)
XLA Ops:
  0.6 10.6 %shard_map.77 = (bf16[16,16,16,128]{3,2,1,0:T(8,128)(2,1)S(1)}, bf16[18,18,16,128]{3,2,1,0:T(8,128)(2,1)S(1)}, bf16[7,128,128]{2,1,0:T(8,128)(2,1)S(1)}, f32[128...) custom-call(bf16[16,16,16,128]{3,2,1,0:T(8,128)(2,1)} %x_hbm.1, ...), custom_call_target="tpu_custom_call" | custom-call | flops 939524096 | bytes 2097152 | tf_op jit(solution)/shard_map/pallas_call | solution.py:374
  11.2 1.3 %shard_map.78 = (bf16[16,16,16,128]{3,2,1,0:T(8,128)(2,1)}, f32[128,128]{1,0:T(8,128)}) custom-call(bf16[16,16,16,128]{3,2,1,0:T(8,128)(2,1)S(1)} %get-tuple-element.11.inner, bf16[18,18,16,128]{3,2,1,0:T(8,128)(2,1)S(1)} %get-tuple-element.12.px, bf16[7,128,128]{2,1,0:T(8,128)(2,1)S(1)} %get-tuple-element.13.cw, f32[128,128]{1,0:T(8,128)S(1)} %get-tuple-element.14.scale, ...), custom_call_target="tpu_custom_call" | custom-call | tf_op jit(solution)/shard_map/pallas_call | solution.py:432

commit v8 on v7

--- a/solution.py
+++ b/solution.py
@@ -87,7 +87,7 @@
     x_hbm, c_hbm, lf_hbm, sc_hbm, live_hbm, tn_hbm,
     out_ref, px, cw, scale, prior, nodes_in, received,
     lf, sc, live, tn,
-    face, face_stage, stage, x0, edge, halo0,
+    side, face, face_stage, stage, x0, edge, halo0,
     lf_stage, lf_edge, lf_halo, lf_corner, field, once,
     nodes_out, pick, picked,
     local_sem, h0_send, h0_recv, hx_send, hx_recv, lf_send, lf_recv, lc_send, lc_recv,
@@ -173,15 +173,14 @@
     layer_copies = [
         remote(edge.at[d], halo0.at[d], h0_send.at[d], h0_recv.at[d], to[d]) for d in range(4)
     ]
-    x_edges = [x_hbm.at[0], x_hbm.at[rows - 1], x_hbm.at[:, 0], x_hbm.at[:, cols - 1]]
     x_halos = [
         px.at[rows + 1, pl.ds(1, cols)],
         px.at[0, pl.ds(1, cols)],
-        px.at[pl.ds(1, rows), cols + 1],
-        px.at[pl.ds(1, rows), 0],
+        side.at[0],
+        side.at[1],
     ]
     x_copies = [
-        remote(x_edges[d], x_halos[d], hx_send.at[d], hx_recv.at[d], to[d]) for d in range(4)
+        remote(face.at[d], x_halos[d], hx_send.at[d], hx_recv.at[d], to[d]) for d in range(4)
     ]
     two = 2 * tile_b
     lf_srcs = [lf_edge.at[0], lf_edge.at[1], lf_edge.at[2, pl.ds(0, 2 * tile_a)], lf_edge.at[3, pl.ds(0, 2 * tile_a)]]
@@ -341,8 +340,14 @@
     prior[...] = stencil(once, 1, tile_a, 8, tile_b).reshape(tile_nodes, width)
     scale[...] = jnp.exp(lf[...])
 
-    for d in range(4):
+    def side_halo(d):
+        x_copies[d].wait_recv()
+        px[halo_at[d]] = side[d - 2]
+
+    for d in range(2):
         pl.when(has_from[d])(x_copies[d].wait_recv)
+    for d in range(2, 4):
+        pl.when(has_from[d])(functools.partial(side_halo, d))
     for copy in node_receives + block_receives:
         copy.wait_recv()
     def sent(d):
@@ -389,6 +394,7 @@
                 vmem((1, faces), jnp.int32),
                 vmem((1, ny), jnp.int32),
                 vmem((ny, slots), jnp.int32),
+                vmem((2, rows, layers, width), BF),
                 vmem((4, rows, layers, width), BF),
                 vmem((4 * rows * 8, width), F32),
                 vmem((faces * 8, width), F32),

time: 12.7 us -> 12.6 us (level)
  no operation moved by 1% of the time
where the time goes in v8:
time: 12.6 us; the launch traced here: 12.4 us
  Pallas kernels  11.8 us (94%)
  between operations  0.64 us (5%)
    pallas_call x1, Pallas kernels, per_device(): pl.pallas_call(functools.partial(kernel, nx, ny), out_shape=(shape(adjoin...  10.5 us
    pallas_call x1, Pallas kernels, per_device(): pl.pallas_call(functools.partial(finish, ny), out_shape=(shape(adjoint_tr...  1.34 us

profile of v8, /device:TPU:9, one launch (start us, length us, event | category | flops | bytes accessed | tf_op | source)
XLA Modules:
  0.0 12.4 jit_solution(9420339467483625320)
XLA Ops:
  0.6 10.5 %shard_map.77 = (bf16[16,16,16,128]{3,2,1,0:T(8,128)(2,1)S(1)}, bf16[18,18,16,128]{3,2,1,0:T(8,128)(2,1)S(1)}, bf16[7,128,128]{2,1,0:T(8,128)(2,1)S(1)}, f32[128...) custom-call(bf16[16,16,16,128]{3,2,1,0:T(8,128)(2,1)} %x_hbm.1, ...), custom_call_target="tpu_custom_call" | custom-call | flops 939524096 | bytes 2097152 | tf_op jit(solution)/shard_map/pallas_call | solution.py:379
  11.1 1.3 %shard_map.78 = (bf16[16,16,16,128]{3,2,1,0:T(8,128)(2,1)}, f32[128,128]{1,0:T(8,128)}) custom-call(bf16[16,16,16,128]{3,2,1,0:T(8,128)(2,1)S(1)} %get-tuple-element.11.inner, bf16[18,18,16,128]{3,2,1,0:T(8,128)(2,1)S(1)} %get-tuple-element.12.px, bf16[7,128,128]{2,1,0:T(8,128)(2,1)S(1)} %get-tuple-element.13.cw, f32[128,128]{1,0:T(8,128)S(1)} %get-tuple-element.14.scale, ...), custom_call_target="tpu_custom_call" | custom-call | tf_op jit(solution)/shard_map/pallas_call | solution.py:438

commit v9 on v8

--- a/solution.py
+++ b/solution.py
@@ -139,8 +139,8 @@
 
     partners = ny - 1 + (one(low_a) + one(high_a)) * (1 + one(low_b) + one(high_b))
 
-    for load in loads:
-        load.start()
+    for n in (0, 1, 2, 3, 5, 4, 6, 7, 8, 9):
+        loads[n].start()
 
     def zero_when(flag, ref, index):
         @pl.when(jnp.logical_not(flag))
@@ -199,13 +199,24 @@
         def _():
             copy.start()
 
+    loads[5].wait()
+    lf_edge[0] = lf[0:two].astype(BF)
+    lf_edge[1] = lf[tile_nodes - two : tile_nodes].astype(BF)
+    for d, first in ((2, 0), (3, tile_b - 2)):
+        for c in range(2):
+            lf_stage[c * tile_a : (c + 1) * tile_a] = lf[pl.ds(first + c, tile_a, stride=tile_b), :]
+        lf_edge[d, 0 : 2 * tile_a] = lf_stage[...].astype(BF)
+
     pl.semaphore_wait(barrier, partners)
     for d in range(4):
         start_when(has_to[d], layer_copies[d])
     for d in range(4):
+        start_when(has_to[d], lf_copies[d])
+    for d in range(4):
+        start_when(corner_has_to[d], corner_copies[d])
+    for d in range(4):
         start_when(has_to[d], x_copies[d])
 
-    loads[5].wait()
     loads[6].wait()
     loads[7].wait()
     slot_id = lax.broadcasted_iota(jnp.int32, (1, slots), 1)
@@ -231,19 +242,8 @@
     )
     nodes_in[j] = nodes_out[j]
 
-    lf_edge[0] = lf[0:two].astype(BF)
-    lf_edge[1] = lf[tile_nodes - two : tile_nodes].astype(BF)
-    for d, first in ((2, 0), (3, tile_b - 2)):
-        for c in range(2):
-            lf_stage[c * tile_a : (c + 1) * tile_a] = lf[pl.ds(first + c, tile_a, stride=tile_b), :]
-        lf_edge[d, 0 : 2 * tile_a] = lf_stage[...].astype(BF)
-
     for copy in node_sends:
         copy.start()
-    for d in range(4):
-        start_when(has_to[d], lf_copies[d])
-    for d in range(4):
-        start_when(corner_has_to[d], corner_copies[d])
 
     loads[4].wait()
     stage[...] = px[inner_a, inner_b].astype(F32)[:, :, 0:8, :].reshape(faces * 8, width)

time: 12.6 us -> 12.6 us (level)
  no operation moved by 1% of the time
where the time goes in v9:
time: 12.6 us; the launch traced here: 12.5 us
  Pallas kernels  11.8 us (94%)
  between operations  0.64 us (5%)
    pallas_call x1, Pallas kernels, per_device(): pl.pallas_call(functools.partial(kernel, nx, ny), out_shape=(shape(adjoin...  10.5 us
    pallas_call x1, Pallas kernels, per_device(): pl.pallas_call(functools.partial(finish, ny), out_shape=(shape(adjoint_tr...  1.34 us

profile of v9, /device:TPU:9, one launch (start us, length us, event | category | flops | bytes accessed | tf_op | source)
XLA Modules:
  0.0 12.5 jit_solution(15800872978838195149)
XLA Ops:
  0.6 10.5 %shard_map.77 = (bf16[16,16,16,128]{3,2,1,0:T(8,128)(2,1)S(1)}, bf16[18,18,16,128]{3,2,1,0:T(8,128)(2,1)S(1)}, bf16[7,128,128]{2,1,0:T(8,128)(2,1)S(1)}, f32[128...) custom-call(bf16[16,16,16,128]{3,2,1,0:T(8,128)(2,1)} %x_hbm.1, ...), custom_call_target="tpu_custom_call" | custom-call | flops 939524096 | bytes 2097152 | tf_op jit(solution)/shard_map/pallas_call | solution.py:379
  11.1 1.3 %shard_map.78 = (bf16[16,16,16,128]{3,2,1,0:T(8,128)(2,1)}, f32[128,128]{1,0:T(8,128)}) custom-call(bf16[16,16,16,128]{3,2,1,0:T(8,128)(2,1)S(1)} %get-tuple-element.11.inner, bf16[18,18,16,128]{3,2,1,0:T(8,128)(2,1)S(1)} %get-tuple-element.12.px, bf16[7,128,128]{2,1,0:T(8,128)(2,1)S(1)} %get-tuple-element.13.cw, f32[128,128]{1,0:T(8,128)S(1)} %get-tuple-element.14.scale, ...), custom_call_target="tpu_custom_call" | custom-call | tf_op jit(solution)/shard_map/pallas_call | solution.py:438
